TPU v7x, 32 devices: a whole 2x2x4 slice. The times are simulated.
32 devices in a mesh: pool: 2 (over y), inst: 4 (over z), tp: 4 (over x, core).
Axes of the slice: x: 2, y: 2, z: 4, core: 2. Of those that a mesh axis runs over, the one named last changes fastest.
Arguments:
- prefill_q: bfloat16 [8, 768, 8, 1024], P(('pool', 'inst'), None, 'tp'), parts along dimension 0, may hold values from -8 to 8
- prefill_kv: bfloat16 [8, 2, 768, 8, 128], P(('pool', 'inst'), None, None, 'tp'), parts along dimension 0, may hold values from -8 to 8
- span_len: int32 [8], P(('pool', 'inst')), parts along dimension 0, may hold values from 1 to 768, as said below
- page_seg: int32 [8, 24], P(('pool', 'inst')), parts along dimension 0, may hold values from 0 to 12, as said below
- page_dest: int32 [8, 24, 1], P(('pool', 'inst')), parts along dimension 0, may hold values from 0 to 3, as said below
- page_row: int32 [8, 24], P(('pool', 'inst')), parts along dimension 0, may hold values from 0 to 15, as said below
- dec_q: bfloat16 [8, 16, 2, 8, 1024], P(('pool', 'inst'), None, None, 'tp'), parts along dimension 0, may hold values from -8 to 8
- dec_new: bfloat16 [8, 16, 2, 2, 8, 128], P(('pool', 'inst'), None, None, None, 'tp'), parts along dimension 0, may hold values from -6 to 6
- cache_kv: bfloat16 [8, 64, 2, 32, 8, 128], P(('pool', 'inst'), None, None, None, 'tp'), parts along dimension 0, may hold values from -8 to 8
- block_table: int32 [8, 64], P(('pool', 'inst')), parts along dimension 0, may hold values from 0 to 63, each once within a row
- cache_len: int32 [8, 16], P(('pool', 'inst')), parts along dimension 0, may hold values from 2 to 128, as said below
Outputs:
- prefill_out: bfloat16 [8, 768, 8, 1024], P(('pool', 'inst'), None, 'tp'), parts along dimension 0
- dec_out: bfloat16 [8, 16, 2, 8, 1024], P(('pool', 'inst'), None, None, 'tp'), parts along dimension 0
There are 2 independent parts, one for each index of `pool`. A program takes and returns all parts, laid end to end along the dimension named above; each array names one. Nothing has to cross between parts.
Inputs may be any that keep to these rules, and one draw needn't show every extreme that they name: `span_len`: some instance's block is full. `page_seg`: never falls along a block, starts at 0 and rises by one from request to request; each request holds 1 to 12 whole pages, and the first request of every block exactly 12. `page_dest`: all pages of one request go to one decode instance; from one instance at most 12 pages go to one decode instance, and exactly that many in every instance. `page_row`: all pages of one request join one row. `block_table`: each instance's row holds each of its pool pages once. `cache_len`: some row holds 128 tokens.
All inputs are finite; a program needn't handle non-finite values.
Results may differ from a plain program's by a relative error of at most 0.0033.
Values may be sent and summed in bfloat16 or wider, within the bound.
No kernel may reach another device: no remote copies, remote signals or barrier semaphores. Data moves between devices by JAX's collectives and lax.ppermute only.
A program may use at most 128 MiB of HBM per device.

v0:
```python
import functools
import math

import jax
import jax.numpy as jnp
from jax import lax
from jax.experimental import pallas as pl
from jax.experimental.pallas import tpu as pltpu
from jax.sharding import PartitionSpec as P

NEGATIVE = -1e30
LOG2E = math.log2(math.e)
LANES = 128
DIRECT = 8
VMEM_LIMIT = 48 * 1024 * 1024

SMEM_SPEC = pl.BlockSpec(memory_space=pltpu.SMEM)
HBM_SPEC = pl.BlockSpec(memory_space=pltpu.HBM)
VMEM_SPEC = pl.BlockSpec(memory_space=pltpu.VMEM)


def query_rows(field):
    lead = math.prod(field.shape[:-2])
    heads, width = field.shape[-2:]
    split = field.reshape(lead, heads, width // LANES, LANES)
    return split.transpose(0, 2, 1, 3).reshape(-1, LANES)


def from_rows(rows, shape):
    heads, width = shape[-2:]
    lead = math.prod(shape[:-2])
    split = rows.reshape(lead, width // LANES, heads, LANES)
    return split.transpose(0, 2, 1, 3).reshape(shape)


def head_of(shape, axis, heads):
    return lax.broadcasted_iota(jnp.int32, shape, axis) % heads


def dot_nt(first, second):
    return lax.dot_general(
        first, second, (((1,), (1,)), ((), ())), preferred_element_type=jnp.float32
    )


def dot_nn(first, second):
    return jnp.dot(first, second, preferred_element_type=jnp.float32)


def two_terms(weights):
    upper = weights.astype(jnp.bfloat16)
    lower = (weights - upper.astype(jnp.float32)).astype(jnp.bfloat16)
    return jnp.concatenate([upper, lower], axis=0)


def spread_heads(rows, heads):
    if heads == 1:
        return rows
    owner = head_of((16, LANES), 0, heads)
    tall = rows.reshape(-1, 16, LANES)
    parts = []
    for h in range(heads):
        mark = jnp.where(owner == h, 1.0, 0.0).astype(rows.dtype)
        parts.append((tall * mark[None]).reshape(rows.shape))
    return jnp.concatenate(parts, axis=1)


def pick_head(wide, heads):
    if heads == 1:
        return wide
    owner = head_of((wide.shape[0], LANES), 0, heads)
    picked = wide[:, :LANES]
    for h in range(1, heads):
        picked = jnp.where(owner == h, wide[:, h * LANES : (h + 1) * LANES], picked)
    return picked


def cache_kernel(
    sizes, len_ref, seg_hbm, dest_hbm, row_hbm, table_hbm, clen_hbm,
    q_hbm, fresh_hbm, pool_hbm, kv_hbm,
    info_ref, part_ref, lse_ref, keys_ref, vals_ref, own_q_ref,
    seg_ref, dest_ref, row_ref, table_ref, clen_ref,
    fresh_ref, pool_ref, kv_ref, scr_ref, sems,
):
    heads, page, pages, rows, steps, pages_max, requests = sizes
    copies = [
        pltpu.make_async_copy(source, target, sems.at[i])
        for i, (source, target) in enumerate((
            (seg_hbm, seg_ref), (dest_hbm, dest_ref), (row_hbm, row_ref),
            (kv_hbm, kv_ref), (table_hbm, table_ref), (clen_hbm, clen_ref),
            (q_hbm, own_q_ref), (fresh_hbm, fresh_ref.at[: fresh_hbm.shape[0]]),
            (pool_hbm, pool_ref),
        ))
    ]
    if fresh_ref.shape[0] > fresh_hbm.shape[0]:
        fresh_ref[fresh_hbm.shape[0] :, :] = jnp.zeros(
            (fresh_ref.shape[0] - fresh_hbm.shape[0], LANES), fresh_ref.dtype
        )
    for copy in copies:
        copy.start()
    span = pages * page

    for r in range(info_ref.shape[1]):
        info_ref[0, r] = 0
        info_ref[1, r] = 0
        info_ref[2, r] = -1
        info_ref[3, r] = 0
    for copy in copies[:3]:
        copy.wait()
    length = len_ref[0]
    info_ref[5, 0] = length

    def note(p, _):
        r = seg_ref[0, p]
        fresh_request = jnp.logical_or(p == 0, r != seg_ref[0, jnp.maximum(p - 1, 0)])

        @pl.when(fresh_request)
        def _():
            info_ref[0, r] = p * page
            info_ref[2, r] = jnp.where(p * page < length, dest_ref[0, p], -1)
            info_ref[3, r] = row_ref[0, p]

        info_ref[1, r] = jnp.minimum((p + 1) * page, length)
        info_ref[4, p] = info_ref[0, r]
        return 0

    lax.fori_loop(0, pages, note, 0)

    copies[3].wait()
    for part, out_ref in enumerate((keys_ref, vals_ref)):
        if heads == 1:
            out_ref[...] = kv_ref[part * span : (part + 1) * span, :]
        else:
            scr_ref[...] = kv_ref[part * span * heads : (part + 1) * span * heads, :].astype(
                jnp.float32
            )
            for h in range(heads):
                out_ref[:, h * LANES : (h + 1) * LANES] = scr_ref[
                    pl.ds(h, span, stride=heads), :
                ].astype(jnp.bfloat16)

    for copy in copies[4:]:
        copy.wait()
    scale2 = LANES**-0.5 * LOG2E
    per_row = own_q_ref.shape[0] // rows
    groups = per_row // (steps * heads)
    fresh = fresh_ref[...]
    width = fresh.shape[0]
    page_rows = page * heads

    col = lax.broadcasted_iota(jnp.int32, (per_row, width), 1)
    sub = lax.broadcasted_iota(jnp.int32, (per_row, width), 0)
    fresh_ok = (
        ((col // heads) % 2 == 0)
        & ((col // (2 * heads)) % steps <= sub // (groups * heads))
        & (col % heads == sub % heads)
    )
    fresh_row = jnp.where(fresh_ok, col // (2 * heads * steps), -1)
    ccol = lax.broadcasted_iota(jnp.int32, (per_row, pages_max * page_rows), 1)
    csub = lax.broadcasted_iota(jnp.int32, (per_row, pages_max * page_rows), 0)
    far = rows * pages_max * page
    token = jnp.where(ccol % heads == csub % heads, ccol // heads, far)

    def gather(b, part):
        pieces = []
        for j in range(pages_max):
            spot = (table_ref[0, b * pages_max + j] * 2 + part) * page_rows
            pieces.append(pool_ref[pl.ds(pl.multiple_of(spot, page_rows), page_rows), :])
        return jnp.concatenate(pieces, axis=0)

    def row_slice(b):
        return slice(b * per_row, (b + 1) * per_row)

    fresh_scores = [dot_nt(own_q_ref[row_slice(b), :], fresh) for b in range(rows)]
    scores = [dot_nt(own_q_ref[row_slice(b), :], gather(b, 0)) for b in range(rows)]
    cache_terms, fresh_terms, totals = [], [], []
    for b in range(rows):
        s_c = jnp.where(token < clen_ref[0, b], scores[b], NEGATIVE)
        s_f = jnp.where(fresh_row == b, fresh_scores[b], NEGATIVE)
        pieces = [s_c[:, i : i + width] for i in range(0, s_c.shape[1], width)] + [s_f]
        top = functools.reduce(jnp.maximum, pieces)
        top = jnp.max(top, axis=1, keepdims=True)
        weights = [jnp.exp2((piece - top) * scale2) for piece in pieces]
        total = jnp.sum(functools.reduce(jnp.add, weights), axis=1, keepdims=True)
        cache_terms.append(two_terms(jnp.concatenate(weights[:-1], axis=1)))
        fresh_terms.append(pltpu.roll(weights[-1], heads, 1))
        totals.append(total)
        lse = top * scale2 + jnp.log2(total)
        lse_ref[row_slice(b), :] = jnp.broadcast_to(lse, (per_row, LANES))
    count = rows * per_row
    fresh_acc = dot_nn(two_terms(jnp.concatenate(fresh_terms, axis=0)), fresh)
    fresh_acc = fresh_acc[:count] + fresh_acc[count:]
    for b in range(rows):
        acc = dot_nn(cache_terms[b], gather(b, 1))
        acc = acc[:per_row] + acc[per_row:] + fresh_acc[row_slice(b)]
        part_ref[row_slice(b), :] = acc * (1.0 / totals[b])


def pages_kernel(sizes, per_slot, info_ref, *refs):
    heads, page, pages, rows, steps, pages_max, requests, instances = sizes
    slot_count = instances // per_slot
    slots = refs[:slot_count]
    keys_ref, vals_ref, own_ref, send_ref, q_scr = refs[slot_count:]
    me = lax.axis_index("inst")
    per_row = slots[0].shape[0] // (per_slot * rows)
    span = pages * page
    scale2 = LANES**-0.5 * LOG2E
    for r in range(requests):
        slot = lax.rem(me - info_ref[2, r] + instances, instances)
        row = info_ref[3, r]
        if slot_count == 1:
            start = pl.multiple_of((slot * rows + row) * per_row, per_row)
            q_scr[r * per_row : (r + 1) * per_row, :] = slots[0][pl.ds(start, per_row), :]
        else:
            start = pl.multiple_of(row * per_row, per_row)
            for k in range(slot_count):

                @pl.when(slot == k)
                def _():
                    q_scr[r * per_row : (r + 1) * per_row, :] = slots[k][pl.ds(start, per_row), :]

    scores = dot_nt(spread_heads(q_scr[...], heads), keys_ref[...])
    token = lax.broadcasted_iota(jnp.int32, (per_row, span), 1)
    weights, tops, totals = [], [], []
    for r in range(requests):
        keep = (token >= info_ref[0, r]) & (token < info_ref[1, r])
        s_r = jnp.where(keep, scores[r * per_row : (r + 1) * per_row], NEGATIVE)
        top = jnp.max(s_r, axis=1, keepdims=True)
        w_r = jnp.where(keep, jnp.exp2((s_r - top) * scale2), 0.0)
        weights.append(w_r)
        tops.append(top)
        totals.append(jnp.sum(w_r, axis=1, keepdims=True))
    count = requests * per_row
    acc = dot_nn(two_terms(jnp.concatenate(weights, axis=0)), vals_ref[...])
    acc = pick_head(acc[:count] + acc[count:], heads)
    total = jnp.concatenate(totals, axis=0)
    live = total > 0.0
    blended = jnp.where(live, acc / jnp.where(live, total, 1.0), 0.0)
    lse = jnp.where(
        live,
        jnp.concatenate(tops, axis=0) * scale2 + jnp.log2(jnp.where(live, total, 1.0)),
        NEGATIVE,
    )
    own_ref[...] = blended
    send_ref[:count, :] = blended.astype(jnp.bfloat16)
    blocks = -(-count // LANES)
    lines = []
    for j in range(blocks):
        piece = lse[j * LANES : min((j + 1) * LANES, count)]
        shape = (piece.shape[0], LANES)
        same = lax.broadcasted_iota(jnp.int32, shape, 0) == lax.broadcasted_iota(
            jnp.int32, shape, 1
        )
        lines.append(jnp.sum(jnp.where(same, piece, 0.0), axis=0, keepdims=True))
    line = jnp.concatenate(lines, axis=0)
    first = line.astype(jnp.bfloat16)
    rest = line - first.astype(jnp.float32)
    second = rest.astype(jnp.bfloat16)
    third = (rest - second.astype(jnp.float32)).astype(jnp.bfloat16)
    terms = [t.astype(jnp.float32) for t in (first, second, third)]
    lane = lax.broadcasted_iota(jnp.int32, (1, LANES), 1)
    for f in (2, 3):
        tags = jnp.full((1, LANES), -1, jnp.int32)
        for r in range(requests):
            tags = jnp.where(lane == r, info_ref[f, r], tags)
        terms.append(tags.astype(jnp.float32))
    spare = send_ref.shape[0] - count
    terms.append(jnp.zeros((spare - 3 * blocks - 2, LANES), jnp.float32))
    send_ref[count:, :] = jnp.concatenate(terms, axis=0).astype(jnp.bfloat16)


def prefill_kernel(sizes, info_ref, q_ref, keys_ref, vals_ref, after_ref, out_ref, lag_ref):
    heads, page, pages, block = sizes
    tile = pl.program_id(0)
    page_rows = out_ref.shape[0] * page // block
    per_token = page_rows // page
    per_block = block // page
    scale2 = LANES**-0.5 * LOG2E
    length = info_ref[5, 0]

    @pl.when(tile == 0)
    def _():
        lane = lax.broadcasted_iota(jnp.int32, lag_ref.shape, 1)
        lag_ref[...] = lane - lax.broadcasted_iota(jnp.int32, lag_ref.shape, 0) // per_token

    first_key = info_ref[4, tile * per_block]
    first_block = first_key // block
    behind = tile - first_block

    def attend(count):
        base = (tile - (count - 1)) * block
        keys = keys_ref[pl.ds(pl.multiple_of(base, block), count * block), :]
        vals = vals_ref[pl.ds(pl.multiple_of(base, block), count * block), :]
        lane = lax.broadcasted_iota(jnp.int32, (1, block), 1)
        def score(p):
            rows = slice(p * page_rows, (p + 1) * page_rows)
            return dot_nt(spread_heads(q_ref[rows, :], heads), keys)

        ahead = score(0)
        for p in range(per_block):
            rows = slice(p * page_rows, (p + 1) * page_rows)
            scores = ahead
            if p + 1 < per_block:
                ahead = score(p + 1)
            start = info_ref[4, tile * per_block + p] - base
            pieces = []
            for j in range(count):
                s_j = scores[:, j * block : (j + 1) * block]
                keep = lane >= start - j * block
                if j == count - 1:
                    keep = keep & (lag_ref[...] <= p * page)
                pieces.append(jnp.where(keep, s_j, NEGATIVE))
            top = pieces[0]
            for piece in pieces[1:]:
                top = jnp.maximum(top, piece)
            top = jnp.max(top, axis=1, keepdims=True)
            weights = [jnp.exp2((piece - top) * scale2) for piece in pieces]
            total = weights[0]
            for w_j in weights[1:]:
                total = total + w_j
            total = jnp.sum(total, axis=1, keepdims=True)
            joined = jnp.concatenate([w_j.astype(jnp.bfloat16) for w_j in weights], axis=1)
            acc = pick_head(dot_nn(joined, vals), heads)
            place = lax.broadcasted_iota(jnp.int32, (page_rows, 1), 0) // per_token
            live = place < length - (tile * block + p * page)
            out_ref[rows, :] = (acc * jnp.where(live, 1.0 / total, 0.0)).astype(jnp.bfloat16)

    longest = 3
    for count in range(1, longest + 1):
        pl.when(behind == count - 1)(functools.partial(attend, count))


def join_kernel(sizes, per_slot, *refs):
    heads, rows, requests, instances = sizes
    slot_count = instances // per_slot
    own_ref = refs[0]
    sent = refs[1 : slot_count + 1]
    part_ref, lse_ref, out_ref, top_scr, total_scr, acc_scr, tag_scr, tags, sem = refs[slot_count + 1 :]
    me = lax.axis_index("inst")
    per_row = part_ref.shape[0] // rows
    count = requests * per_row
    blocks = -(-count // LANES)
    tall = sent[0].shape[0] // per_slot
    lines = []
    for n in range(instances):
        k, i = divmod(n, per_slot)
        stats = sent[k][i * tall + count : (i + 1) * tall, :].astype(jnp.float32)
        lines.append(
            stats[:blocks] + stats[blocks : 2 * blocks] + stats[2 * blocks : 3 * blocks]
        )
        tag_scr[n : n + 1, :] = stats[3 * blocks : 3 * blocks + 1].astype(jnp.int32)
        tag_scr[instances + n : instances + n + 1, :] = stats[
            3 * blocks + 1 : 3 * blocks + 2
        ].astype(jnp.int32)
    copy = pltpu.make_async_copy(tag_scr, tags, sem)
    copy.start()
    top_scr[...] = lse_ref[...]
    total_scr[...] = jnp.ones_like(total_scr)
    acc_scr[...] = part_ref[...]
    lane = lax.broadcasted_iota(jnp.int32, (per_row, LANES), 1)
    sub = lax.broadcasted_iota(jnp.int32, (per_row, LANES), 0)
    copy.wait()
    for n in range(instances):
        k, i = divmod(n, per_slot)
        for r in range(requests):

            @pl.when(tags[n, r] == me)
            def _():
                start = pl.multiple_of(tags[instances + n, r] * per_row, per_row)
                place = pl.ds(start, per_row)
                j, offset = divmod(r * per_row, LANES)
                spread = jnp.where(lane == sub + offset, lines[n][j : j + 1, :], 0.0)
                level = jnp.sum(spread, axis=1, keepdims=True)
                spot = r * per_row
                if n == 0:
                    values = own_ref[spot : spot + per_row, :]
                else:
                    spot = spot + i * tall
                    values = sent[k][spot : spot + per_row, :].astype(jnp.float32)
                top = top_scr[place, :]
                joined = jnp.maximum(top, level)
                old = jnp.exp2(top - joined)
                new = jnp.exp2(level - joined)
                top_scr[place, :] = joined
                total_scr[place, :] = total_scr[place, :] * old + new
                acc_scr[place, :] = acc_scr[place, :] * old + values * new

    out_ref[...] = (acc_scr[...] / total_scr[...]).astype(jnp.bfloat16)


def exchange(block, instances):
    if instances <= DIRECT:
        slots = [block]
        for k in range(1, instances):
            slots.append(
                lax.ppermute(block, "inst", [(i, (i + k) % instances) for i in range(instances)])
            )
        return slots
    whole = lax.all_gather(block, "inst", axis=0)
    order = lax.rem(lax.axis_index("inst") - jnp.arange(instances) + instances, instances)
    return [jnp.take(whole, order, axis=0).reshape((-1,) + block.shape[1:])]


def in_hbm(field):
    return pltpu.with_memory_space_constraint(field, pltpu.HBM)


def params(**extra):
    return pltpu.CompilerParams(vmem_limit_bytes=VMEM_LIMIT, **extra)


def shards(
    instances,
    prefill_q,
    prefill_kv,
    span_len,
    page_seg,
    page_dest,
    page_row,
    dec_q,
    dec_new,
    cache_kv,
    block_table,
    cache_len,
):
    _, span, heads, width = prefill_q.shape
    pages = page_seg.shape[1]
    _, rows, steps = dec_q.shape[:3]
    pool, page = cache_kv.shape[1], cache_kv.shape[3]
    pages_max = block_table.shape[1] // rows
    capacity = -(-2 * pages // instances)
    requests = pages - capacity + 1
    groups = width // LANES
    per_row = steps * groups * heads
    block = LANES
    sizes = (heads, page, pages, rows, steps, pages_max, requests)
    dest = page_dest.reshape(1, pages)
    slot_width = 32
    f32, bf16, i32 = jnp.float32, jnp.bfloat16, jnp.int32
    shape = jax.ShapeDtypeStruct

    queries = query_rows(dec_q[0])
    q_slots = exchange(queries, instances)
    per_slot = instances // len(q_slots)

    fresh = dec_new.reshape(-1, LANES)
    source_kv = prefill_kv.reshape(-1, LANES)
    cache = cache_kv.reshape(-1, LANES)
    ints = (page_seg, dest, page_row, block_table, cache_len)
    info, part, lse, keys, vals, own_q = pl.pallas_call(
        functools.partial(cache_kernel, sizes),
        out_shape=(
            shape((8, slot_width), i32),
            shape((rows * per_row, LANES), f32),
            shape((rows * per_row, LANES), f32),
            shape((span, heads * LANES), bf16),
            shape((span, heads * LANES), bf16),
            shape(queries.shape, bf16),
        ),
        in_specs=[SMEM_SPEC] + [HBM_SPEC] * 9,
        out_specs=(SMEM_SPEC,) + (VMEM_SPEC,) * 5,
        scratch_shapes=[pltpu.SMEM(x.shape, i32) for x in ints]
        + [
            pltpu.VMEM((-(-fresh.shape[0] // LANES) * LANES, LANES), bf16),
            pltpu.VMEM(cache.shape, bf16),
            pltpu.VMEM(source_kv.shape, bf16),
            pltpu.VMEM((span * heads, LANES), f32),
            pltpu.SemaphoreType.DMA((9,)),
        ],
        compiler_params=params(),
        name="cache",
    )(span_len, *map(in_hbm, (*ints, queries, fresh, cache, source_kv)))
    q_slots = [own_q] + q_slots[1:] if per_slot == 1 else q_slots

    count = requests * per_row
    tall = count + -(-(3 * -(-count // LANES) + 2) // 16) * 16
    own, sent = pl.pallas_call(
        functools.partial(pages_kernel, sizes + (instances,), per_slot),
        out_shape=(shape((count, LANES), f32), shape((tall, LANES), bf16)),
        in_specs=[SMEM_SPEC] + [VMEM_SPEC] * (len(q_slots) + 2),
        out_specs=(VMEM_SPEC, VMEM_SPEC),
        scratch_shapes=[pltpu.VMEM((count, LANES), bf16)],
        compiler_params=params(),
        name="pages",
    )(info, *q_slots, keys, vals)
    sent_slots = exchange(sent, instances)

    q_rows = query_rows(prefill_q[0])
    tile_rows = block * groups * heads
    tiles = span // block
    whole = lambda i: (0, 0)
    prefill_out = pl.pallas_call(
        functools.partial(prefill_kernel, (heads, page, pages, block)),
        out_shape=shape(q_rows.shape, bf16),
        grid=(tiles,),
        in_specs=[SMEM_SPEC]
        + [
            pl.BlockSpec((tile_rows, LANES), lambda i: (i, 0)),
            pl.BlockSpec(keys.shape, whole),
            pl.BlockSpec(vals.shape, whole),
            pl.BlockSpec(memory_space=pl.ANY),
        ],
        out_specs=pl.BlockSpec((tile_rows, LANES), lambda i: (i, 0)),
        scratch_shapes=[pltpu.VMEM((page * groups * heads, block), i32)],
        compiler_params=params(),
        name="prefill",
    )(info, q_rows, keys, vals, own)

    dec_out = pl.pallas_call(
        functools.partial(join_kernel, (heads, rows, requests, instances), per_slot),
        out_shape=shape((rows * per_row, LANES), bf16),
        in_specs=[VMEM_SPEC] * (3 + len(sent_slots)),
        out_specs=VMEM_SPEC,
        scratch_shapes=[pltpu.VMEM((rows * per_row, LANES), f32)] * 3
        + [
            pltpu.VMEM((-(-2 * instances // 8) * 8, LANES), i32),
            pltpu.SMEM((-(-2 * instances // 8) * 8, LANES), i32),
            pltpu.SemaphoreType.DMA,
        ],
        compiler_params=params(),
        name="join",
    )(own, *sent_slots, part, lse)

    return (
        from_rows(prefill_out, prefill_q.shape),
        from_rows(dec_out, dec_q.shape),
    )


def solution(mesh):
    return jax.shard_map(
        functools.partial(shards, mesh.shape["inst"]),
        mesh=mesh,
        in_specs=(
            P(("pool", "inst"), None, "tp", None),
            P(("pool", "inst"), None, None, "tp", None),
            P(("pool", "inst")),
            P(("pool", "inst"), None),
            P(("pool", "inst"), None, None),
            P(("pool", "inst"), None),
            P(("pool", "inst"), None, None, "tp", None),
            P(("pool", "inst"), None, None, None, "tp", None),
            P(("pool", "inst"), None, None, None, "tp", None),
            P(("pool", "inst"), None),
            P(("pool", "inst"), None),
        ),
        out_specs=(
            P(("pool", "inst"), None, "tp", None),
            P(("pool", "inst"), None, None, "tp", None),
        ),
        check_vma=False,
    )
```

profile of v0, /device:TPU:0, one launch (start us, length us, event | category | flops | bytes accessed | tf_op | source)
XLA Modules:
  0.0 34.1 jit_solution(911211843095353267)
XLA Ops:
  0.6 0.0 copy-start
  0.6 5.1 %collective-permute-start.2 = (bf16[512,128]{1,0:T(8,128)(2,1)}, bf16[512,128]{1,0:T(8,128)(2,1)S(1)}, u32[]{:S(2)}, u32[]{:S(2)}) collective-permute-start(bf16[512,128]{1,0:T(8,128)(2,1)} %bitcast.28), channel_id=1, source_target_pairs={{0,12},{4,0},{8,4},{12,8},{1,13},{5,1},{9,5},{13,9},{2,14},{6,2},{... | collective-permute-start | bytes 393224 | tf_op jit(solution)/shard_map/ppermute | solution.py:396
  5.7 0.0 collective-permute-start.1
  5.7 1.0 %collective-permute-start = (bf16[512,128]{1,0:T(8,128)(2,1)}, bf16[512,128]{1,0:T(8,128)(2,1)S(1)}, u32[]{:S(2)}, u32[]{:S(2)}) collective-permute-start(bf16[512,128]{1,0:T(8,128)(2,1)} %bitcast.30), channel_id=1, source_target_pairs={{0,4},{4,8},{8,12},{12,0},{1,5},{5,9},{9,13},{13,1},{2,6},{6,10},{... | collective-permute-start | bytes 393224 | tf_op jit(solution)/shard_map/ppermute | solution.py:396
  7.4 3.7 %cache.1 = (s32[8,32]{1,0:T(8,128)S(1)}, f32[512,128]{1,0:T(8,128)S(1)}, f32[512,128]{1,0:T(8,128)S(1)}, bf16[768,256]{1,0:T(8,128)(2,1)S(1)}, bf16[768,256]{1,0...) custom-call(s32[1]{0:T(128)S(6)} %copy.17.len_ref, s32[1,24]{1,0:T(1,128)} %seg_hbm.1, s32[1,24]{1,0:T(1,128)} %bitcast.34, ...), custom_call_target="tpu_custom_call" | custom-call | tf_op jit(solution)/shard_map/cache/pallas_call | solution.py:450
  11.1 0.0 collective-permute-done.2.refs_3_
  11.2 6.0 %collective-permute-done.1.refs_2_ = bf16[512,128]{1,0:T(8,128)(2,1)S(1)} collective-permute-done((bf16[512,128]{1,0:T(8,128)(2,1)}, bf16[512,128]{1,0:T(8,128)(2,1)S(1)}, u32[]{:S(2)}, u32[]{:S(2)}) %collective-permute-start.1) | collective-permute-done | bytes 131104 | tf_op jit(solution)/shard_map/ppermute | solution.py:396
  17.2 0.0 collective-permute-done.refs_1_
  17.2 2.2 %pages.1 = (f32[416,128]{1,0:T(8,128)S(1)}, bf16[432,128]{1,0:T(8,128)(2,1)S(1)}) custom-call(s32[8,32]{1,0:T(8,128)S(1)} %get-tuple-element.10.info_ref, bf16[512,128]{1,0:T(8,128)(2,1)S(1)} %get-tuple-element.13.refs_0_, bf16[512,128]{1,0:T(8,128)(2,1)S(1)} %collective-permute-done.refs_1_, bf16[512,128]{1,0:T(8,128)(2,1)S(1)} %collective-permute-done.1.refs_2_, ...), custom_call_target="tpu_custom_call" | custom-call | tf_op jit(solution)/shard_map/pages/pallas_call | solution.py:477
  19.4 1.7 %collective-permute-start.5 = (bf16[432,128]{1,0:T(8,128)(2,1)S(1)}, bf16[432,128]{1,0:T(8,128)(2,1)S(1)}, u32[]{:S(2)}, u32[]{:S(2)}) collective-permute-start(bf16[432,128]{1,0:T(8,128)(2,1)S(1)} %get-tuple-element.15.refs_1_), channel_id=1, source_target_pairs={{0,12},{4,0},{8,4},{12,8},{1,13},{5,1},{9,5},{13,9},{2,14},{6,2},{... | collective-permute-start | bytes 331784 | tf_op jit(solution)/shard_map/ppermute | solution.py:396
  21.0 1.1 %collective-permute-start.4 = (bf16[432,128]{1,0:T(8,128)(2,1)S(1)}, bf16[432,128]{1,0:T(8,128)(2,1)S(1)}, u32[]{:S(2)}, u32[]{:S(2)}) collective-permute-start(bf16[432,128]{1,0:T(8,128)(2,1)S(1)} %get-tuple-element.15.refs_1_), channel_id=1, source_target_pairs={{0,8},{4,12},{8,0},{12,4},{1,9},{5,13},{9,1},{13,5},{2,10},{6,14},... | collective-permute-start | bytes 331784 | tf_op jit(solution)/shard_map/ppermute | solution.py:396
  22.1 1.9 %collective-permute-start.3 = (bf16[432,128]{1,0:T(8,128)(2,1)S(1)}, bf16[432,128]{1,0:T(8,128)(2,1)S(1)}, u32[]{:S(2)}, u32[]{:S(2)}) collective-permute-start(bf16[432,128]{1,0:T(8,128)(2,1)S(1)} %get-tuple-element.15.refs_1_), channel_id=1, source_target_pairs={{0,4},{4,8},{8,12},{12,0},{1,5},{5,9},{9,13},{13,1},{2,6},{6,10},{... | collective-permute-start | bytes 331784 | tf_op jit(solution)/shard_map/ppermute | solution.py:396
  24.1 0.0 copy-done
  24.1 8.1 %prefill.1 = bf16[12288,128]{1,0:T(8,128)(2,1)} custom-call(s32[8,32]{1,0:T(8,128)S(1)} %get-tuple-element.10.info_ref, bf16[12288,128]{1,0:T(8,128)(2,1)S(1)} %bitcast.24, bf16[768,256]{1,0:T(8,128)(2,1)S(1)} %get-tuple-element.11.refs_4_.keys_ref, bf16[768,256]{1,0:T(8,128)(2,1)S(1)} %get-tuple-element.12.refs_5_.vals_ref, ...), custom_call_target="tpu_custom_call" | custom-call | tf_op jit(solution)/shard_map/prefill/pallas_call | solution.py:492
  32.1 0.0 collective-permute-done.5.refs_4_
  32.1 0.0 collective-permute-done.4.refs_3_
  32.1 0.0 collective-permute-done.3.refs_2_
  32.1 1.9 %join.1 = bf16[512,128]{1,0:T(8,128)(2,1)} custom-call(f32[416,128]{1,0:T(8,128)S(1)} %get-tuple-element.14.after_ref.refs_0_, bf16[432,128]{1,0:T(8,128)(2,1)S(1)} %get-tuple-element.15.refs_1_, bf16[432,128]{1,0:T(8,128)(2,1)S(1)} %collective-permute-done.3.refs_2_, bf16[432,128]{1,0:T(8,128)(2,1)S(1)} %collective-permute-done.4.refs_3_, ...), custom_call_target="tpu_custom_call" | custom-call | tf_op jit(solution)/shard_map/join/pallas_call | solution.py:509
Async XLA Ops:
  0.6 23.4 %copy-start = (bf16[1,768,2,1024]{3,2,1,0:T(2,128)(2,1)S(1)}, bf16[1,768,2,1024]{3,2,1,0:T(2,128)(2,1)}, u32[]{:S(2)}) copy-start(bf16[1,768,2,1024]{3,2,1,0:T(2,128)(2,1)} %param.11) | copy-start | bytes 9437188
  0.6 10.5 %collective-permute-start.2 = (bf16[512,128]{1,0:T(8,128)(2,1)}, bf16[512,128]{1,0:T(8,128)(2,1)S(1)}, u32[]{:S(2)}, u32[]{:S(2)}) collective-permute-start(bf16[512,128]{1,0:T(8,128)(2,1)} %bitcast.28), channel_id=1, source_target_pairs={{0,12},{4,0},{8,4},{12,8},{1,13},{5,1},{9,5},{13,9},{2,14},{6,2},{... | collective-permute-start | bytes 393224 | tf_op jit(solution)/shard_map/ppermute | solution.py:396
  5.7 11.4 %collective-permute-start.1 = (bf16[512,128]{1,0:T(8,128)(2,1)}, bf16[512,128]{1,0:T(8,128)(2,1)S(1)}, u32[]{:S(2)}, u32[]{:S(2)}) collective-permute-start(bf16[512,128]{1,0:T(8,128)(2,1)} %bitcast.29), channel_id=1, source_target_pairs={{0,8},{4,12},{8,0},{12,4},{1,9},{5,13},{9,1},{13,5},{2,10},{6,14},... | collective-permute-start | bytes 393224 | tf_op jit(solution)/shard_map/ppermute | solution.py:396
  5.7 11.4 %collective-permute-start = (bf16[512,128]{1,0:T(8,128)(2,1)}, bf16[512,128]{1,0:T(8,128)(2,1)S(1)}, u32[]{:S(2)}, u32[]{:S(2)}) collective-permute-start(bf16[512,128]{1,0:T(8,128)(2,1)} %bitcast.30), channel_id=1, source_target_pairs={{0,4},{4,8},{8,12},{12,0},{1,5},{5,9},{9,13},{13,1},{2,6},{6,10},{... | collective-permute-start | bytes 393224 | tf_op jit(solution)/shard_map/ppermute | solution.py:396
  19.4 12.8 %collective-permute-start.5 = (bf16[432,128]{1,0:T(8,128)(2,1)S(1)}, bf16[432,128]{1,0:T(8,128)(2,1)S(1)}, u32[]{:S(2)}, u32[]{:S(2)}) collective-permute-start(bf16[432,128]{1,0:T(8,128)(2,1)S(1)} %get-tuple-element.15.refs_1_), channel_id=1, source_target_pairs={{0,12},{4,0},{8,4},{12,8},{1,13},{5,1},{9,5},{13,9},{2,14},{6,2},{... | collective-permute-start | bytes 331784 | tf_op jit(solution)/shard_map/ppermute | solution.py:396
  21.0 11.1 %collective-permute-start.4 = (bf16[432,128]{1,0:T(8,128)(2,1)S(1)}, bf16[432,128]{1,0:T(8,128)(2,1)S(1)}, u32[]{:S(2)}, u32[]{:S(2)}) collective-permute-start(bf16[432,128]{1,0:T(8,128)(2,1)S(1)} %get-tuple-element.15.refs_1_), channel_id=1, source_target_pairs={{0,8},{4,12},{8,0},{12,4},{1,9},{5,13},{9,1},{13,5},{2,10},{6,14},... | collective-permute-start | bytes 331784 | tf_op jit(solution)/shard_map/ppermute | solution.py:396
  22.1 10.0 %collective-permute-start.3 = (bf16[432,128]{1,0:T(8,128)(2,1)S(1)}, bf16[432,128]{1,0:T(8,128)(2,1)S(1)}, u32[]{:S(2)}, u32[]{:S(2)}) collective-permute-start(bf16[432,128]{1,0:T(8,128)(2,1)S(1)} %get-tuple-element.15.refs_1_), channel_id=1, source_target_pairs={{0,4},{4,8},{8,12},{12,0},{1,5},{5,9},{9,13},{13,1},{2,6},{6,10},{... | collective-permute-start | bytes 331784 | tf_op jit(solution)/shard_map/ppermute | solution.py:396
where the time goes:
time: 34.5 us; the launch traced here: 34.1 us
  Pallas kernels  15.9 us (46%)
  starting transfers between devices  10.8 us (31%)
  waiting for transfers between devices  6.02 us (17%)
  between operations  1.32 us (4%)
    ppermute x6, starting transfers between devices, exchange(): lax.ppermute(block, 'inst', [(i, (i + k) % instances) for i in range(inst...  10.8 us
    pallas_call x1, Pallas kernels, shards(): pl.pallas_call(functools.partial(prefill_kernel, (heads, page, pages, blo...  8.06 us
    ppermute x6, waiting for transfers between devices, exchange(): lax.ppermute(block, 'inst', [(i, (i + k) % instances) for i in range(inst...  6.02 us
    pallas_call x1, Pallas kernels, shards(): pl.pallas_call(functools.partial(cache_kernel, sizes), out_shape=(shape((...  3.72 us
    pallas_call x1, Pallas kernels, shards(): pl.pallas_call(functools.partial(pages_kernel, sizes + (instances,), per_...  2.19 us
    pallas_call x1, Pallas kernels, shards(): pl.pallas_call(functools.partial(join_kernel, (heads, rows, requests, ins...  1.93 us
  transfers between devices with their start and end apart: 6, of which 1 were waited for; matrix products, arithmetic and copies ran while one was open for 0% of the time, Pallas kernels for 35%

commit v1 on v0

--- a/solution.py
+++ b/solution.py
@@ -12,9 +12,12 @@
 LOG2E = math.log2(math.e)
 LANES = 128
 DIRECT = 8
+EARLY = 2
 VMEM_LIMIT = 48 * 1024 * 1024
 
 SMEM_SPEC = pl.BlockSpec(memory_space=pltpu.SMEM)
+BRIEF = pl.CostEstimate(flops=1000, bytes_accessed=1000, transcendentals=0)
+ANY_SPEC = pl.BlockSpec(memory_space=pl.ANY)
 HBM_SPEC = pl.BlockSpec(memory_space=pltpu.HBM)
 VMEM_SPEC = pl.BlockSpec(memory_space=pltpu.VMEM)
 
@@ -78,7 +81,7 @@
 def cache_kernel(
     sizes, len_ref, seg_hbm, dest_hbm, row_hbm, table_hbm, clen_hbm,
     q_hbm, fresh_hbm, pool_hbm, kv_hbm,
-    info_ref, part_ref, lse_ref, keys_ref, vals_ref, own_q_ref,
+    info_ref, lse_ref, total_ref, part_ref, keys_ref, vals_ref, own_q_ref,
     seg_ref, dest_ref, row_ref, table_ref, clen_ref,
     fresh_ref, pool_ref, kv_ref, scr_ref, sems,
 ):
@@ -98,9 +101,10 @@
         )
     for copy in copies:
         copy.start()
+    total_ref[...] = jnp.ones_like(total_ref)
     span = pages * page
 
-    for r in range(info_ref.shape[1]):
+    for r in range(requests):
         info_ref[0, r] = 0
         info_ref[1, r] = 0
         info_ref[2, r] = -1
@@ -109,22 +113,15 @@
         copy.wait()
     length = len_ref[0]
     info_ref[5, 0] = length
-
-    def note(p, _):
+    for p in reversed(range(pages)):
         r = seg_ref[0, p]
-        fresh_request = jnp.logical_or(p == 0, r != seg_ref[0, jnp.maximum(p - 1, 0)])
-
-        @pl.when(fresh_request)
-        def _():
-            info_ref[0, r] = p * page
-            info_ref[2, r] = jnp.where(p * page < length, dest_ref[0, p], -1)
-            info_ref[3, r] = row_ref[0, p]
-
+        info_ref[0, r] = p * page
+        info_ref[2, r] = jnp.where(p * page < length, dest_ref[0, p], -1)
+        info_ref[3, r] = row_ref[0, p]
+    for p in range(pages):
+        r = seg_ref[0, p]
         info_ref[1, r] = jnp.minimum((p + 1) * page, length)
         info_ref[4, p] = info_ref[0, r]
-        return 0
-
-    lax.fori_loop(0, pages, note, 0)
 
     copies[3].wait()
     for part, out_ref in enumerate((keys_ref, vals_ref)):
@@ -196,43 +193,53 @@
         part_ref[row_slice(b), :] = acc * (1.0 / totals[b])
 
 
-def pages_kernel(sizes, per_slot, info_ref, *refs):
-    heads, page, pages, rows, steps, pages_max, requests, instances = sizes
-    slot_count = instances // per_slot
+def pages_kernel(sizes, partners, info_ref, *refs):
+    heads, page, pages, rows, requests, capacity, instances = sizes
+    slot_count = 1 if partners is None else len(partners)
     slots = refs[:slot_count]
-    keys_ref, vals_ref, own_ref, send_ref, q_scr = refs[slot_count:]
+    keys_ref, vals_ref, _, own_ref, send_ref, token_ref, q_scr = refs[slot_count:]
     me = lax.axis_index("inst")
-    per_row = slots[0].shape[0] // (per_slot * rows)
     span = pages * page
     scale2 = LANES**-0.5 * LOG2E
+    count = own_ref.shape[0]
+    per_row = count // requests
+    token_ref[...] = jnp.zeros_like(token_ref)
     for r in range(requests):
-        slot = lax.rem(me - info_ref[2, r] + instances, instances)
-        row = info_ref[3, r]
-        if slot_count == 1:
-            start = pl.multiple_of((slot * rows + row) * per_row, per_row)
-            q_scr[r * per_row : (r + 1) * per_row, :] = slots[0][pl.ds(start, per_row), :]
+        dest, row = info_ref[2, r], info_ref[3, r]
+        place = slice(r * per_row, (r + 1) * per_row)
+        if partners is None:
+            start = pl.multiple_of((jnp.maximum(dest, 0) * rows + row) * per_row, per_row)
+            q_scr[place, :] = slots[0][pl.ds(start, per_row), :]
         else:
             start = pl.multiple_of(row * per_row, per_row)
-            for k in range(slot_count):
-
-                @pl.when(slot == k)
-                def _():
-                    q_scr[r * per_row : (r + 1) * per_row, :] = slots[k][pl.ds(start, per_row), :]
-
-    scores = dot_nt(spread_heads(q_scr[...], heads), keys_ref[...])
-    token = lax.broadcasted_iota(jnp.int32, (per_row, span), 1)
-    weights, tops, totals = [], [], []
-    for r in range(requests):
-        keep = (token >= info_ref[0, r]) & (token < info_ref[1, r])
-        s_r = jnp.where(keep, scores[r * per_row : (r + 1) * per_row], NEGATIVE)
-        top = jnp.max(s_r, axis=1, keepdims=True)
-        w_r = jnp.where(keep, jnp.exp2((s_r - top) * scale2), 0.0)
-        weights.append(w_r)
-        tops.append(top)
-        totals.append(jnp.sum(w_r, axis=1, keepdims=True))
-    count = requests * per_row
-    acc = dot_nn(two_terms(jnp.concatenate(weights, axis=0)), vals_ref[...])
-    acc = pick_head(acc[:count] + acc[count:], heads)
+            picked = slots[0][pl.ds(start, per_row), :]
+            for k, offset in enumerate(partners[1:]):
+                other = slots[k + 1][pl.ds(start, per_row), :]
+                picked = jnp.where(dest == jnp.bitwise_xor(me, offset), other, picked)
+            q_scr[place, :] = picked
+
+    cut = capacity * page
+    totals, tops, accs = [], [], []
+    for low, high, first, last in ((0, cut, 0, 1), (cut, span, 1, requests)):
+        wide = high - low
+        scores = dot_nt(
+            spread_heads(q_scr[first * per_row : last * per_row, :], heads), keys_ref[low:high, :]
+        )
+        token = low + lax.broadcasted_iota(jnp.int32, (per_row, wide), 1)
+        weights = []
+        for r in range(first, last):
+            keep = (token >= info_ref[0, r]) & (token < info_ref[1, r])
+            spot = (r - first) * per_row
+            s_r = jnp.where(keep, scores[spot : spot + per_row], NEGATIVE)
+            top = jnp.max(s_r, axis=1, keepdims=True)
+            w_r = jnp.where(keep, jnp.exp2((s_r - top) * scale2), 0.0)
+            weights.append(w_r)
+            tops.append(top)
+            totals.append(jnp.sum(w_r, axis=1, keepdims=True))
+        acc = dot_nn(two_terms(jnp.concatenate(weights, axis=0)), vals_ref[low:high, :])
+        half = (last - first) * per_row
+        accs.append(pick_head(acc[:half] + acc[half:], heads))
+    acc = jnp.concatenate(accs, axis=0)
     total = jnp.concatenate(totals, axis=0)
     live = total > 0.0
     blended = jnp.where(live, acc / jnp.where(live, total, 1.0), 0.0)
@@ -269,16 +276,18 @@
     send_ref[count:, :] = jnp.concatenate(terms, axis=0).astype(jnp.bfloat16)
 
 
-def prefill_kernel(sizes, info_ref, q_ref, keys_ref, vals_ref, after_ref, out_ref, lag_ref):
+def prefill_kernel(sizes, first_tile, info_ref, q_ref, keys_ref, vals_ref, *refs):
     heads, page, pages, block = sizes
-    tile = pl.program_id(0)
+    out_ref, token_ref, lag_ref = refs[-3:]
+    tile = pl.program_id(0) + first_tile
+    token_ref[...] = jnp.zeros_like(token_ref)
     page_rows = out_ref.shape[0] * page // block
     per_token = page_rows // page
     per_block = block // page
     scale2 = LANES**-0.5 * LOG2E
     length = info_ref[5, 0]
 
-    @pl.when(tile == 0)
+    @pl.when(tile == first_tile)
     def _():
         lane = lax.broadcasted_iota(jnp.int32, lag_ref.shape, 1)
         lag_ref[...] = lane - lax.broadcasted_iota(jnp.int32, lag_ref.shape, 0) // per_token
@@ -330,20 +339,28 @@
         pl.when(behind == count - 1)(functools.partial(attend, count))
 
 
-def join_kernel(sizes, per_slot, *refs):
-    heads, rows, requests, instances = sizes
-    slot_count = instances // per_slot
-    own_ref = refs[0]
-    sent = refs[1 : slot_count + 1]
-    part_ref, lse_ref, out_ref, top_scr, total_scr, acc_scr, tag_scr, tags, sem = refs[slot_count + 1 :]
+def join_kernel(sizes, with_own, last, *refs):
+    rows, requests, blocks_of = sizes
+    sent_count = len(blocks_of)
+    refs = list(refs)
+    own_ref = refs.pop(0) if with_own else None
+    sent, refs = refs[:sent_count], refs[sent_count:]
+    top_in, total_in, acc_in = refs[:3]
+    refs = refs[4:]
+    if last:
+        out_ref, top_scr, total_scr, acc_scr, tag_scr, tags, sem = refs
+    else:
+        top_scr, total_scr, acc_scr, token_ref, tag_scr, tags, sem = refs
+        token_ref[...] = jnp.zeros_like(token_ref)
     me = lax.axis_index("inst")
-    per_row = part_ref.shape[0] // rows
+    per_row = acc_in.shape[0] // rows
     count = requests * per_row
     blocks = -(-count // LANES)
-    tall = sent[0].shape[0] // per_slot
+    instances = sum(blocks_of)
+    places = [(k, i) for k in range(sent_count) for i in range(blocks_of[k])]
     lines = []
-    for n in range(instances):
-        k, i = divmod(n, per_slot)
+    for n, (k, i) in enumerate(places):
+        tall = sent[k].shape[0] // blocks_of[k]
         stats = sent[k][i * tall + count : (i + 1) * tall, :].astype(jnp.float32)
         lines.append(
             stats[:blocks] + stats[blocks : 2 * blocks] + stats[2 * blocks : 3 * blocks]
@@ -354,14 +371,14 @@
         ].astype(jnp.int32)
     copy = pltpu.make_async_copy(tag_scr, tags, sem)
     copy.start()
-    top_scr[...] = lse_ref[...]
-    total_scr[...] = jnp.ones_like(total_scr)
-    acc_scr[...] = part_ref[...]
+    top_scr[...] = top_in[...]
+    total_scr[...] = total_in[...]
+    acc_scr[...] = acc_in[...]
     lane = lax.broadcasted_iota(jnp.int32, (per_row, LANES), 1)
     sub = lax.broadcasted_iota(jnp.int32, (per_row, LANES), 0)
     copy.wait()
-    for n in range(instances):
-        k, i = divmod(n, per_slot)
+    for n, (k, i) in enumerate(places):
+        tall = sent[k].shape[0] // blocks_of[k]
         for r in range(requests):
 
             @pl.when(tags[n, r] == me)
@@ -372,7 +389,7 @@
                 spread = jnp.where(lane == sub + offset, lines[n][j : j + 1, :], 0.0)
                 level = jnp.sum(spread, axis=1, keepdims=True)
                 spot = r * per_row
-                if n == 0:
+                if with_own and n == 0:
                     values = own_ref[spot : spot + per_row, :]
                 else:
                     spot = spot + i * tall
@@ -385,20 +402,17 @@
                 total_scr[place, :] = total_scr[place, :] * old + new
                 acc_scr[place, :] = acc_scr[place, :] * old + values * new
 
-    out_ref[...] = (acc_scr[...] / total_scr[...]).astype(jnp.bfloat16)
-
-
-def exchange(block, instances):
-    if instances <= DIRECT:
-        slots = [block]
-        for k in range(1, instances):
-            slots.append(
-                lax.ppermute(block, "inst", [(i, (i + k) % instances) for i in range(instances)])
-            )
-        return slots
+    if last:
+        out_ref[...] = (acc_scr[...] / total_scr[...]).astype(jnp.bfloat16)
+
+
+def swap(block, offset, instances):
+    return lax.ppermute(block, "inst", [(i, i ^ offset) for i in range(instances)])
+
+
+def gather_all(block):
     whole = lax.all_gather(block, "inst", axis=0)
-    order = lax.rem(lax.axis_index("inst") - jnp.arange(instances) + instances, instances)
-    return [jnp.take(whole, order, axis=0).reshape((-1,) + block.shape[1:])]
+    return whole.reshape((-1,) + block.shape[1:])
 
 
 def in_hbm(field):
@@ -439,26 +453,26 @@
     f32, bf16, i32 = jnp.float32, jnp.bfloat16, jnp.int32
     shape = jax.ShapeDtypeStruct
 
+    direct = instances <= DIRECT and instances & (instances - 1) == 0
     queries = query_rows(dec_q[0])
-    q_slots = exchange(queries, instances)
-    per_slot = instances // len(q_slots)
+    if direct:
+        arrived = {x: swap(queries, x, instances) for x in range(1, instances)}
 
     fresh = dec_new.reshape(-1, LANES)
     source_kv = prefill_kv.reshape(-1, LANES)
     cache = cache_kv.reshape(-1, LANES)
     ints = (page_seg, dest, page_row, block_table, cache_len)
-    info, part, lse, keys, vals, own_q = pl.pallas_call(
+    info, *state, keys, vals, own_q = pl.pallas_call(
         functools.partial(cache_kernel, sizes),
         out_shape=(
             shape((8, slot_width), i32),
-            shape((rows * per_row, LANES), f32),
-            shape((rows * per_row, LANES), f32),
+            *[shape((rows * per_row, LANES), f32)] * 3,
             shape((span, heads * LANES), bf16),
             shape((span, heads * LANES), bf16),
             shape(queries.shape, bf16),
         ),
         in_specs=[SMEM_SPEC] + [HBM_SPEC] * 9,
-        out_specs=(SMEM_SPEC,) + (VMEM_SPEC,) * 5,
+        out_specs=(SMEM_SPEC,) + (VMEM_SPEC,) * 6,
         scratch_shapes=[pltpu.SMEM(x.shape, i32) for x in ints]
         + [
             pltpu.VMEM((-(-fresh.shape[0] // LANES) * LANES, LANES), bf16),
@@ -468,58 +482,94 @@
             pltpu.SemaphoreType.DMA((9,)),
         ],
         compiler_params=params(),
+        cost_estimate=BRIEF,
         name="cache",
     )(span_len, *map(in_hbm, (*ints, queries, fresh, cache, source_kv)))
-    q_slots = [own_q] + q_slots[1:] if per_slot == 1 else q_slots
-
     count = requests * per_row
     tall = count + -(-(3 * -(-count // LANES) + 2) // 16) * 16
-    own, sent = pl.pallas_call(
-        functools.partial(pages_kernel, sizes + (instances,), per_slot),
-        out_shape=(shape((count, LANES), f32), shape((tall, LANES), bf16)),
-        in_specs=[SMEM_SPEC] + [VMEM_SPEC] * (len(q_slots) + 2),
-        out_specs=(VMEM_SPEC, VMEM_SPEC),
-        scratch_shapes=[pltpu.VMEM((count, LANES), bf16)],
-        compiler_params=params(),
-        name="pages",
-    )(info, *q_slots, keys, vals)
-    sent_slots = exchange(sent, instances)
+    token = shape((8, LANES), f32)
+
+    def attend_pages(partners, slots, after):
+        return pl.pallas_call(
+            functools.partial(
+                pages_kernel,
+                (heads, page, pages, rows, requests, capacity, instances),
+                partners,
+            ),
+            out_shape=(shape((count, LANES), f32), shape((tall, LANES), bf16), token),
+            in_specs=[SMEM_SPEC] + [VMEM_SPEC] * (len(slots) + 2) + [ANY_SPEC],
+            out_specs=(VMEM_SPEC,) * 3,
+            scratch_shapes=[pltpu.VMEM((count, LANES), bf16)],
+            compiler_params=params(),
+            cost_estimate=BRIEF,
+            name="pages",
+        )(info, *slots, keys, vals, after)
 
     q_rows = query_rows(prefill_q[0])
     tile_rows = block * groups * heads
     tiles = span // block
     whole = lambda i: (0, 0)
-    prefill_out = pl.pallas_call(
-        functools.partial(prefill_kernel, (heads, page, pages, block)),
-        out_shape=shape(q_rows.shape, bf16),
-        grid=(tiles,),
-        in_specs=[SMEM_SPEC]
-        + [
-            pl.BlockSpec((tile_rows, LANES), lambda i: (i, 0)),
-            pl.BlockSpec(keys.shape, whole),
-            pl.BlockSpec(vals.shape, whole),
-            pl.BlockSpec(memory_space=pl.ANY),
-        ],
-        out_specs=pl.BlockSpec((tile_rows, LANES), lambda i: (i, 0)),
-        scratch_shapes=[pltpu.VMEM((page * groups * heads, block), i32)],
-        compiler_params=params(),
-        name="prefill",
-    )(info, q_rows, keys, vals, own)
-
-    dec_out = pl.pallas_call(
-        functools.partial(join_kernel, (heads, rows, requests, instances), per_slot),
-        out_shape=shape((rows * per_row, LANES), bf16),
-        in_specs=[VMEM_SPEC] * (3 + len(sent_slots)),
-        out_specs=VMEM_SPEC,
-        scratch_shapes=[pltpu.VMEM((rows * per_row, LANES), f32)] * 3
-        + [
-            pltpu.VMEM((-(-2 * instances // 8) * 8, LANES), i32),
-            pltpu.SMEM((-(-2 * instances // 8) * 8, LANES), i32),
-            pltpu.SemaphoreType.DMA,
-        ],
-        compiler_params=params(),
-        name="join",
-    )(own, *sent_slots, part, lse)
+
+    def attend_source(first, last, after, earlier=None):
+        rest = [after] if earlier is None else [after, earlier]
+        return pl.pallas_call(
+            functools.partial(prefill_kernel, (heads, page, pages, block), first),
+            out_shape=(shape(q_rows.shape, bf16), token),
+            grid=(last - first,),
+            in_specs=[SMEM_SPEC]
+            + [
+                pl.BlockSpec((tile_rows, LANES), lambda i: (i + first, 0)),
+                pl.BlockSpec(keys.shape, whole),
+                pl.BlockSpec(vals.shape, whole),
+            ]
+            + [ANY_SPEC] * len(rest),
+            out_specs=(
+                pl.BlockSpec((tile_rows, LANES), lambda i: (i + first, 0)),
+                pl.BlockSpec(token.shape, whole),
+            ),
+            scratch_shapes=[pltpu.VMEM((page * groups * heads, block), i32)],
+            input_output_aliases={} if earlier is None else {5: 0},
+            compiler_params=params(),
+            cost_estimate=BRIEF,
+            name="prefill",
+        )(info, q_rows, keys, vals, *rest)
+
+    def join(own, sent, state, after, last):
+        blocks_of = tuple(block.shape[0] // tall for block in sent)
+        tag_rows = -(-2 * sum(blocks_of) // 8) * 8
+        lead = [] if own is None else [own]
+        whole_state = [shape((rows * per_row, LANES), f32)] * 3
+        result = shape((rows * per_row, LANES), bf16)
+        return pl.pallas_call(
+            functools.partial(join_kernel, (rows, requests, blocks_of), own is not None, last),
+            out_shape=result if last else (*whole_state, token),
+            in_specs=[VMEM_SPEC] * (len(lead) + len(sent) + 3) + [ANY_SPEC],
+            out_specs=VMEM_SPEC if last else (VMEM_SPEC,) * 4,
+            scratch_shapes=[pltpu.VMEM(x.shape, f32) for x in whole_state if last]
+            + [
+                pltpu.VMEM((tag_rows, LANES), i32),
+                pltpu.SMEM((tag_rows, LANES), i32),
+                pltpu.SemaphoreType.DMA,
+            ],
+            compiler_params=params(),
+            cost_estimate=BRIEF,
+            name="join",
+        )(*lead, *sent, *state, after)
+
+    if direct and instances > 2:
+        x, *near = range(instances - 1, 0, -1)
+        own, block_own, done = attend_pages((0, x), [own_q, arrived[x]], state[0])
+        far = swap(block_own, x, instances)
+        prefill_out, done = attend_source(0, EARLY, done)
+        _, sent, done = attend_pages(tuple(near), [arrived[x] for x in near], done)
+        *state, done = join(own, [block_own, far], state, done, False)
+        prefill_out, done = attend_source(EARLY, tiles, done, prefill_out)
+        dec_out = join(None, [swap(sent, x, instances) for x in near], state, done, True)
+    else:
+        queries = gather_all(queries)
+        own, sent, done = attend_pages(None, [queries], state[0])
+        prefill_out, done = attend_source(0, tiles, done)
+        dec_out = join(None, [gather_all(sent)], state, done, True)
 
     return (
         from_rows(prefill_out, prefill_q.shape),

time: 34.5 us -> 33.8 us (0.980)
  waiting for transfers between devices: 6.02 us -> 0.59 us
  Pallas kernels: 15.9 us -> 20.5 us
  starting transfers between devices: 10.8 us -> 11.2 us
    ppermute x6, waiting for transfers between devices: 6.02 us -> 0.59 us  [swap(): lax.ppermute(block, 'inst', [(i, i ^ offset) for i in range(instances)])]
    pallas_call x3 -> x6, Pallas kernels: 12.2 us -> 16.8 us  [the longest x2 9.86 us: attend_source(): pl.pallas_call(functools.partial(prefill_kernel, (heads, page, pages, blo...]
  transfers between devices with their start and end apart: 6 -> 6, of which waited for: 1 -> 1; matrix products, arithmetic and copies ran while one was open for 0% -> 0% of each run, Pallas kernels for 35% -> 55%
where the time goes in v1:
time: 33.8 us; the launch traced here: 33.6 us
  Pallas kernels  20.5 us (61%)
  starting transfers between devices  11.2 us (33%)
  between operations  1.33 us (4%)
  waiting for transfers between devices  0.59 us (2%)
    ppermute x6, starting transfers between devices, swap(): lax.ppermute(block, 'inst', [(i, i ^ offset) for i in range(instances)])  11.2 us
    pallas_call x2, Pallas kernels, attend_source(): pl.pallas_call(functools.partial(prefill_kernel, (heads, page, pages, blo...  9.86 us
    pallas_call x2, Pallas kernels, attend_pages(): pl.pallas_call(functools.partial(pages_kernel, (heads, page, pages, rows,...  4.04 us
    pallas_call x1, Pallas kernels, shards(): pl.pallas_call(functools.partial(cache_kernel, sizes), out_shape=(shape((...  3.73 us
    pallas_call x2, Pallas kernels, join(): pl.pallas_call(functools.partial(join_kernel, (rows, requests, blocks_of)...  2.86 us
  transfers between devices with their start and end apart: 6, of which 1 were waited for; matrix products, arithmetic and copies ran while one was open for 0% of the time, Pallas kernels for 55%

profile of v1, /device:TPU:0, one launch (start us, length us, event | category | flops | bytes accessed | tf_op | source)
XLA Modules:
  0.0 33.6 jit_solution(6022347974063150311)
XLA Ops:
  0.6 0.0 copy-start
  0.6 5.1 %collective-permute-start = (bf16[512,128]{1,0:T(8,128)(2,1)}, bf16[512,128]{1,0:T(8,128)(2,1)S(1)}, u32[]{:S(2)}, u32[]{:S(2)}) collective-permute-start(bf16[512,128]{1,0:T(8,128)(2,1)} %bitcast.29), channel_id=1, source_target_pairs={{0,12},{4,8},{8,4},{12,0},{1,13},{5,9},{9,5},{13,1},{2,14},{6,10},... | collective-permute-start | bytes 393224 | tf_op jit(solution)/shard_map/ppermute | solution.py:410
  5.8 0.0 collective-permute-start.3
  5.8 0.6 %collective-permute-start.2 = (bf16[512,128]{1,0:T(8,128)(2,1)}, bf16[512,128]{1,0:T(8,128)(2,1)S(1)}, u32[]{:S(2)}, u32[]{:S(2)}) collective-permute-start(bf16[512,128]{1,0:T(8,128)(2,1)} %bitcast.31), channel_id=1, source_target_pairs={{0,8},{4,12},{8,0},{12,4},{1,9},{5,13},{9,1},{13,5},{2,10},{6,14},... | collective-permute-start | bytes 393224 | tf_op jit(solution)/shard_map/ppermute | solution.py:410
  7.1 3.7 %cache.1 = (s32[8,32]{1,0:T(8,128)S(1)}, f32[512,128]{1,0:T(8,128)S(1)}, f32[512,128]{1,0:T(8,128)S(1)}, f32[512,128]{1,0:T(8,128)S(1)}, bf16[768,256]{1,0:T(8,1...) custom-call(s32[1]{0:T(128)S(6)} %copy.19.len_ref, s32[1,24]{1,0:T(1,128)} %seg_hbm.1, ...), custom_call_target="tpu_custom_call" | custom-call | flops 1000 | bytes 1000 | tf_op jit(solution)/shard_map/cache/pallas_call | solution.py:465
  10.8 0.0 collective-permute-done.refs_1_
  10.8 1.7 %pages.2 = (f32[416,128]{1,0:T(8,128)S(1)}, bf16[432,128]{1,0:T(8,128)(2,1)S(1)}, f32[8,128]{1,0:T(8,128)S(1)}) custom-call(s32[8,32]{1,0:T(8,128)S(1)} %get-tuple-element.22.info_ref, bf16[512,128]{1,0:T(8,128)(2,1)S(1)} %get-tuple-element.25.refs_0_, bf16[512,128]{1,0:T(8,128)(2,1)S(1)} %collective-permute-done.refs_1_, ...), custom_call_target="tpu_custom_call" | custom-call | flops 1000 | bytes 1000 | tf_op jit(solution)/shard_map/pages/pallas_call | solution.py:493
  12.5 3.8 %collective-permute-start.1 = (bf16[432,128]{1,0:T(8,128)(2,1)S(1)}, bf16[432,128]{1,0:T(8,128)(2,1)S(1)}, u32[]{:S(2)}, u32[]{:S(2)}) collective-permute-start(bf16[432,128]{1,0:T(8,128)(2,1)S(1)} %get-tuple-element.28.refs_1_), channel_id=1, source_target_pairs={{0,12},{4,8},{8,4},{12,0},{1,13},{5,9},{9,5},{13,1},{2,14},{6,10},... | collective-permute-start | bytes 331784 | tf_op jit(solution)/shard_map/ppermute | solution.py:410
  16.3 0.0 copy-done
  16.3 3.5 %prefill.2 = (bf16[12288,128]{1,0:T(8,128)(2,1)}, f32[8,128]{1,0:T(8,128)S(1)}) custom-call(s32[8,32]{1,0:T(8,128)S(1)} %get-tuple-element.22.info_ref, bf16[12288,128]{1,0:T(8,128)(2,1)S(1)} %bitcast.24, bf16[768,256]{1,0:T(8,128)(2,1)S(1)} %get-tuple-element.23.refs_2_.keys_ref, bf16[768,256]{1,0:T(8,128)(2,1)S(1)} %get-tuple-element.24.refs_3_.vals_ref, ...), custom_call_target="tpu_custom_call" | custom-call | flops 1000 | bytes 1000 | tf_op jit(solution)/shard_map/prefill/pallas_call | solution.py:515
  19.8 0.0 collective-permute-done.3.refs_1_
  19.8 0.6 %collective-permute-done.2.refs_0_ = bf16[512,128]{1,0:T(8,128)(2,1)S(1)} collective-permute-done((bf16[512,128]{1,0:T(8,128)(2,1)}, bf16[512,128]{1,0:T(8,128)(2,1)S(1)}, u32[]{:S(2)}, u32[]{:S(2)}) %collective-permute-start.2) | collective-permute-done | bytes 131104 | tf_op jit(solution)/shard_map/ppermute | solution.py:410
  20.4 2.4 %pages.3 = (f32[416,128]{1,0:T(8,128)}, bf16[432,128]{1,0:T(8,128)(2,1)S(1)}, f32[8,128]{1,0:T(8,128)S(1)}) custom-call(s32[8,32]{1,0:T(8,128)S(1)} %get-tuple-element.22.info_ref, bf16[512,128]{1,0:T(8,128)(2,1)S(1)} %collective-permute-done.2.refs_0_, bf16[512,128]{1,0:T(8,128)(2,1)S(1)} %collective-permute-done.3.refs_1_, ...), custom_call_target="tpu_custom_call" | custom-call | flops 1000 | bytes 1000 | tf_op jit(solution)/shard_map/pages/pallas_call | solution.py:493
  22.7 0.0 collective-permute-start.5
  22.7 1.6 %collective-permute-start.4 = (bf16[432,128]{1,0:T(8,128)(2,1)S(1)}, bf16[432,128]{1,0:T(8,128)(2,1)S(1)}, u32[]{:S(2)}, u32[]{:S(2)}) collective-permute-start(bf16[432,128]{1,0:T(8,128)(2,1)S(1)} %get-tuple-element.37), channel_id=1, source_target_pairs={{0,8},{4,12},{8,0},{12,4},{1,9},{5,13},{9,1},{13,5},{2,10},{6,14},... | collective-permute-start | bytes 331784 | tf_op jit(solution)/shard_map/ppermute | solution.py:410
  24.3 0.0 collective-permute-done.1.refs_2_
  24.3 0.9 %join.2 = (f32[512,128]{1,0:T(8,128)S(1)}, f32[512,128]{1,0:T(8,128)S(1)}, f32[512,128]{1,0:T(8,128)S(1)}, f32[8,128]{1,0:T(8,128)S(1)}) custom-call(f32[416,128]{1,0:T(8,128)S(1)} %get-tuple-element.27.refs_0_, bf16[432,128]{1,0:T(8,128)(2,1)S(1)} %get-tuple-element.28.refs_1_, bf16[432,128]{1,0:T(8,128)(2,1)S(1)} %collective-permute-done.1.refs_2_, ...), custom_call_target="tpu_custom_call" | custom-call | flops 1000 | bytes 1000 | tf_op jit(solution)/shard_map/join/pallas_call | solution.py:543
  25.2 6.4 %prefill.3 = (bf16[12288,128]{1,0:T(8,128)(2,1)}, f32[8,128]{1,0:T(8,128)S(1)}) custom-call(s32[8,32]{1,0:T(8,128)S(1)} %get-tuple-element.22.info_ref, bf16[12288,128]{1,0:T(8,128)(2,1)S(1)} %bitcast.25, bf16[768,256]{1,0:T(8,128)(2,1)S(1)} %get-tuple-element.23.refs_2_.keys_ref, ...), custom_call_target="tpu_custom_call", output_to_operand_aliasing={{0}: (5, {})} | custom-call | flops 1000 | bytes 1000 | tf_op jit(solution)/shard_map/prefill/pallas_call | solution.py:515
  31.6 0.0 collective-permute-done.5.refs_1_
  31.6 0.0 collective-permute-done.4.refs_0_
  31.6 1.9 %join.3 = bf16[512,128]{1,0:T(8,128)(2,1)} custom-call(bf16[432,128]{1,0:T(8,128)(2,1)S(1)} %collective-permute-done.4.refs_0_, bf16[432,128]{1,0:T(8,128)(2,1)S(1)} %collective-permute-done.5.refs_1_, f32[512,128]{1,0:T(8,128)S(1)} %get-tuple-element.38.refs_2_, f32[512,128]{1,0:T(8,128)S(1)} %get-tuple-element.39.refs_3_, ...), custom_call_target="tpu_custom_call" | custom-call | flops 1000 | bytes 1000 | tf_op jit(solution)/shard_map/join/pallas_call | solution.py:543
Async XLA Ops:
  0.6 15.7 %copy-start = (bf16[1,768,2,1024]{3,2,1,0:T(2,128)(2,1)S(1)}, bf16[1,768,2,1024]{3,2,1,0:T(2,128)(2,1)}, u32[]{:S(2)}) copy-start(bf16[1,768,2,1024]{3,2,1,0:T(2,128)(2,1)} %param.11) | copy-start | bytes 9437188
  0.6 10.1 %collective-permute-start = (bf16[512,128]{1,0:T(8,128)(2,1)}, bf16[512,128]{1,0:T(8,128)(2,1)S(1)}, u32[]{:S(2)}, u32[]{:S(2)}) collective-permute-start(bf16[512,128]{1,0:T(8,128)(2,1)} %bitcast.29), channel_id=1, source_target_pairs={{0,12},{4,8},{8,4},{12,0},{1,13},{5,9},{9,5},{13,1},{2,14},{6,10},... | collective-permute-start | bytes 393224 | tf_op jit(solution)/shard_map/ppermute | solution.py:410
  5.8 14.0 %collective-permute-start.3 = (bf16[512,128]{1,0:T(8,128)(2,1)}, bf16[512,128]{1,0:T(8,128)(2,1)S(1)}, u32[]{:S(2)}, u32[]{:S(2)}) collective-permute-start(bf16[512,128]{1,0:T(8,128)(2,1)} %bitcast.30), channel_id=1, source_target_pairs={{0,4},{4,0},{8,12},{12,8},{1,5},{5,1},{9,13},{13,9},{2,6},{6,2},{1... | collective-permute-start | bytes 393224 | tf_op jit(solution)/shard_map/ppermute | solution.py:410
  5.8 14.6 %collective-permute-start.2 = (bf16[512,128]{1,0:T(8,128)(2,1)}, bf16[512,128]{1,0:T(8,128)(2,1)S(1)}, u32[]{:S(2)}, u32[]{:S(2)}) collective-permute-start(bf16[512,128]{1,0:T(8,128)(2,1)} %bitcast.31), channel_id=1, source_target_pairs={{0,8},{4,12},{8,0},{12,4},{1,9},{5,13},{9,1},{13,5},{2,10},{6,14},... | collective-permute-start | bytes 393224 | tf_op jit(solution)/shard_map/ppermute | solution.py:410
  12.5 11.8 %collective-permute-start.1 = (bf16[432,128]{1,0:T(8,128)(2,1)S(1)}, bf16[432,128]{1,0:T(8,128)(2,1)S(1)}, u32[]{:S(2)}, u32[]{:S(2)}) collective-permute-start(bf16[432,128]{1,0:T(8,128)(2,1)S(1)} %get-tuple-element.28.refs_1_), channel_id=1, source_target_pairs={{0,12},{4,8},{8,4},{12,0},{1,13},{5,9},{9,5},{13,1},{2,14},{6,10},... | collective-permute-start | bytes 331784 | tf_op jit(solution)/shard_map/ppermute | solution.py:410
  22.7 8.9 %collective-permute-start.5 = (bf16[432,128]{1,0:T(8,128)(2,1)S(1)}, bf16[432,128]{1,0:T(8,128)(2,1)S(1)}, u32[]{:S(2)}, u32[]{:S(2)}) collective-permute-start(bf16[432,128]{1,0:T(8,128)(2,1)S(1)} %get-tuple-element.37), channel_id=1, source_target_pairs={{0,4},{4,0},{8,12},{12,8},{1,5},{5,1},{9,13},{13,9},{2,6},{6,2},{1... | collective-permute-start | bytes 331784 | tf_op jit(solution)/shard_map/ppermute | solution.py:410
  22.7 8.9 %collective-permute-start.4 = (bf16[432,128]{1,0:T(8,128)(2,1)S(1)}, bf16[432,128]{1,0:T(8,128)(2,1)S(1)}, u32[]{:S(2)}, u32[]{:S(2)}) collective-permute-start(bf16[432,128]{1,0:T(8,128)(2,1)S(1)} %get-tuple-element.37), channel_id=1, source_target_pairs={{0,8},{4,12},{8,0},{12,4},{1,9},{5,13},{9,1},{13,5},{2,10},{6,14},... | collective-permute-start | bytes 331784 | tf_op jit(solution)/shard_map/ppermute | solution.py:410

commit v2 on v1

--- a/solution.py
+++ b/solution.py
@@ -12,7 +12,7 @@
 LOG2E = math.log2(math.e)
 LANES = 128
 DIRECT = 8
-EARLY = 2
+EARLY = 3
 VMEM_LIMIT = 48 * 1024 * 1024
 
 SMEM_SPEC = pl.BlockSpec(memory_space=pltpu.SMEM)

time: 33.8 us -> 33.1 us (0.979)
  starting transfers between devices: 11.2 us -> 10.3 us
    ppermute x6, starting transfers between devices: 11.2 us -> 10.3 us  [swap(): lax.ppermute(block, 'inst', [(i, i ^ offset) for i in range(instances)])]
  transfers between devices with their start and end apart: 6 -> 6, of which waited for: 1 -> 1; matrix products, arithmetic and copies ran while one was open for 0% -> 0% of each run, Pallas kernels for 55% -> 57%
where the time goes in v2:
time: 33.1 us
  Pallas kernels  20.8 us (63%)
  starting transfers between devices  10.3 us (31%)
  between operations  1.33 us (4%)
  waiting for transfers between devices  0.72 us (2%)
    ppermute x6, starting transfers between devices, swap(): lax.ppermute(block, 'inst', [(i, i ^ offset) for i in range(instances)])  10.3 us
    pallas_call x2, Pallas kernels, attend_source(): pl.pallas_call(functools.partial(prefill_kernel, (heads, page, pages, blo...  9.85 us
    pallas_call x2, Pallas kernels, attend_pages(): pl.pallas_call(functools.partial(pages_kernel, (heads, page, pages, rows,...  4.04 us
    pallas_call x1, Pallas kernels, shards(): pl.pallas_call(functools.partial(cache_kernel, sizes), out_shape=(shape((...  3.73 us
    pallas_call x2, Pallas kernels, join(): pl.pallas_call(functools.partial(join_kernel, (rows, requests, blocks_of)...  3.19 us
    ppermute x6, waiting for transfers between devices, swap(): lax.ppermute(block, 'inst', [(i, i ^ offset) for i in range(instances)])  0.72 us
  transfers between devices with their start and end apart: 6, of which 1 were waited for; matrix products, arithmetic and copies ran while one was open for 0% of the time, Pallas kernels for 57%

profile of v2, /device:TPU:0, one launch (start us, length us, event | category | flops | bytes accessed | tf_op | source)
XLA Modules:
  0.0 33.1 jit_solution(10810769521966111103)
XLA Ops:
  0.6 0.0 copy-start
  0.6 5.1 %collective-permute-start = (bf16[512,128]{1,0:T(8,128)(2,1)}, bf16[512,128]{1,0:T(8,128)(2,1)S(1)}, u32[]{:S(2)}, u32[]{:S(2)}) collective-permute-start(bf16[512,128]{1,0:T(8,128)(2,1)} %bitcast.29), channel_id=1, source_target_pairs={{0,12},{4,8},{8,4},{12,0},{1,13},{5,9},{9,5},{13,1},{2,14},{6,10},... | collective-permute-start | bytes 393224 | tf_op jit(solution)/shard_map/ppermute | solution.py:410
  5.8 0.0 collective-permute-start.3
  5.8 0.6 %collective-permute-start.2 = (bf16[512,128]{1,0:T(8,128)(2,1)}, bf16[512,128]{1,0:T(8,128)(2,1)S(1)}, u32[]{:S(2)}, u32[]{:S(2)}) collective-permute-start(bf16[512,128]{1,0:T(8,128)(2,1)} %bitcast.31), channel_id=1, source_target_pairs={{0,8},{4,12},{8,0},{12,4},{1,9},{5,13},{9,1},{13,5},{2,10},{6,14},... | collective-permute-start | bytes 393224 | tf_op jit(solution)/shard_map/ppermute | solution.py:410
  7.1 3.7 %cache.1 = (s32[8,32]{1,0:T(8,128)S(1)}, f32[512,128]{1,0:T(8,128)S(1)}, f32[512,128]{1,0:T(8,128)S(1)}, f32[512,128]{1,0:T(8,128)S(1)}, bf16[768,256]{1,0:T(8,1...) custom-call(s32[1]{0:T(128)S(6)} %copy.19.len_ref, s32[1,24]{1,0:T(1,128)} %seg_hbm.1, ...), custom_call_target="tpu_custom_call" | custom-call | flops 1000 | bytes 1000 | tf_op jit(solution)/shard_map/cache/pallas_call | solution.py:465
  10.8 0.0 collective-permute-done.refs_1_
  10.8 1.7 %pages.2 = (f32[416,128]{1,0:T(8,128)S(1)}, bf16[432,128]{1,0:T(8,128)(2,1)S(1)}, f32[8,128]{1,0:T(8,128)S(1)}) custom-call(s32[8,32]{1,0:T(8,128)S(1)} %get-tuple-element.22.info_ref, bf16[512,128]{1,0:T(8,128)(2,1)S(1)} %get-tuple-element.25.refs_0_, bf16[512,128]{1,0:T(8,128)(2,1)S(1)} %collective-permute-done.refs_1_, ...), custom_call_target="tpu_custom_call" | custom-call | flops 1000 | bytes 1000 | tf_op jit(solution)/shard_map/pages/pallas_call | solution.py:493
  12.5 3.8 %collective-permute-start.1 = (bf16[432,128]{1,0:T(8,128)(2,1)S(1)}, bf16[432,128]{1,0:T(8,128)(2,1)S(1)}, u32[]{:S(2)}, u32[]{:S(2)}) collective-permute-start(bf16[432,128]{1,0:T(8,128)(2,1)S(1)} %get-tuple-element.28.refs_1_), channel_id=1, source_target_pairs={{0,12},{4,8},{8,4},{12,0},{1,13},{5,9},{9,5},{13,1},{2,14},{6,10},... | collective-permute-start | bytes 331784 | tf_op jit(solution)/shard_map/ppermute | solution.py:410
  16.3 0.0 copy-done
  16.3 5.1 %prefill.2 = (bf16[12288,128]{1,0:T(8,128)(2,1)}, f32[8,128]{1,0:T(8,128)S(1)}) custom-call(s32[8,32]{1,0:T(8,128)S(1)} %get-tuple-element.22.info_ref, bf16[12288,128]{1,0:T(8,128)(2,1)S(1)} %bitcast.24, bf16[768,256]{1,0:T(8,128)(2,1)S(1)} %get-tuple-element.23.refs_2_.keys_ref, bf16[768,256]{1,0:T(8,128)(2,1)S(1)} %get-tuple-element.24.refs_3_.vals_ref, ...), custom_call_target="tpu_custom_call" | custom-call | flops 1000 | bytes 1000 | tf_op jit(solution)/shard_map/prefill/pallas_call | solution.py:515
  21.4 0.0 collective-permute-done.3.refs_1_
  21.4 0.0 collective-permute-done.2.refs_0_
  21.4 2.4 %pages.3 = (f32[416,128]{1,0:T(8,128)}, bf16[432,128]{1,0:T(8,128)(2,1)S(1)}, f32[8,128]{1,0:T(8,128)S(1)}) custom-call(s32[8,32]{1,0:T(8,128)S(1)} %get-tuple-element.22.info_ref, bf16[512,128]{1,0:T(8,128)(2,1)S(1)} %collective-permute-done.2.refs_0_, bf16[512,128]{1,0:T(8,128)(2,1)S(1)} %collective-permute-done.3.refs_1_, ...), custom_call_target="tpu_custom_call" | custom-call | flops 1000 | bytes 1000 | tf_op jit(solution)/shard_map/pages/pallas_call | solution.py:493
  23.8 0.0 collective-permute-start.5
  23.8 0.7 %collective-permute-start.4 = (bf16[432,128]{1,0:T(8,128)(2,1)S(1)}, bf16[432,128]{1,0:T(8,128)(2,1)S(1)}, u32[]{:S(2)}, u32[]{:S(2)}) collective-permute-start(bf16[432,128]{1,0:T(8,128)(2,1)S(1)} %get-tuple-element.37), channel_id=1, source_target_pairs={{0,8},{4,12},{8,0},{12,4},{1,9},{5,13},{9,1},{13,5},{2,10},{6,14},... | collective-permute-start | bytes 331784 | tf_op jit(solution)/shard_map/ppermute | solution.py:410
  24.5 0.0 collective-permute-done.1.refs_2_
  24.5 1.2 %join.2 = (f32[512,128]{1,0:T(8,128)S(1)}, f32[512,128]{1,0:T(8,128)S(1)}, f32[512,128]{1,0:T(8,128)S(1)}, f32[8,128]{1,0:T(8,128)S(1)}) custom-call(f32[416,128]{1,0:T(8,128)S(1)} %get-tuple-element.27.refs_0_, bf16[432,128]{1,0:T(8,128)(2,1)S(1)} %get-tuple-element.28.refs_1_, bf16[432,128]{1,0:T(8,128)(2,1)S(1)} %collective-permute-done.1.refs_2_, ...), custom_call_target="tpu_custom_call" | custom-call | flops 1000 | bytes 1000 | tf_op jit(solution)/shard_map/join/pallas_call | solution.py:543
  25.7 4.7 %prefill.3 = (bf16[12288,128]{1,0:T(8,128)(2,1)}, f32[8,128]{1,0:T(8,128)S(1)}) custom-call(s32[8,32]{1,0:T(8,128)S(1)} %get-tuple-element.22.info_ref, bf16[12288,128]{1,0:T(8,128)(2,1)S(1)} %bitcast.25, bf16[768,256]{1,0:T(8,128)(2,1)S(1)} %get-tuple-element.23.refs_2_.keys_ref, ...), custom_call_target="tpu_custom_call", output_to_operand_aliasing={{0}: (5, {})} | custom-call | flops 1000 | bytes 1000 | tf_op jit(solution)/shard_map/prefill/pallas_call | solution.py:515
  30.4 0.0 collective-permute-done.5.refs_1_
  30.4 0.7 %collective-permute-done.4.refs_0_ = bf16[432,128]{1,0:T(8,128)(2,1)S(1)} collective-permute-done((bf16[432,128]{1,0:T(8,128)(2,1)S(1)}, bf16[432,128]{1,0:T(8,128)(2,1)S(1)}, u32[]{:S(2)}, u32[]{:S(2)}) %collective-permute-start.4) | collective-permute-done | bytes 110624 | tf_op jit(solution)/shard_map/ppermute | solution.py:410
  31.1 2.0 %join.3 = bf16[512,128]{1,0:T(8,128)(2,1)} custom-call(bf16[432,128]{1,0:T(8,128)(2,1)S(1)} %collective-permute-done.4.refs_0_, bf16[432,128]{1,0:T(8,128)(2,1)S(1)} %collective-permute-done.5.refs_1_, f32[512,128]{1,0:T(8,128)S(1)} %get-tuple-element.38.refs_2_, f32[512,128]{1,0:T(8,128)S(1)} %get-tuple-element.39.refs_3_, ...), custom_call_target="tpu_custom_call" | custom-call | flops 1000 | bytes 1000 | tf_op jit(solution)/shard_map/join/pallas_call | solution.py:543
Async XLA Ops:
  0.6 15.7 %copy-start = (bf16[1,768,2,1024]{3,2,1,0:T(2,128)(2,1)S(1)}, bf16[1,768,2,1024]{3,2,1,0:T(2,128)(2,1)}, u32[]{:S(2)}) copy-start(bf16[1,768,2,1024]{3,2,1,0:T(2,128)(2,1)} %param.11) | copy-start | bytes 9437188
  0.6 10.1 %collective-permute-start = (bf16[512,128]{1,0:T(8,128)(2,1)}, bf16[512,128]{1,0:T(8,128)(2,1)S(1)}, u32[]{:S(2)}, u32[]{:S(2)}) collective-permute-start(bf16[512,128]{1,0:T(8,128)(2,1)} %bitcast.29), channel_id=1, source_target_pairs={{0,12},{4,8},{8,4},{12,0},{1,13},{5,9},{9,5},{13,1},{2,14},{6,10},... | collective-permute-start | bytes 393224 | tf_op jit(solution)/shard_map/ppermute | solution.py:410
  5.8 15.7 %collective-permute-start.3 = (bf16[512,128]{1,0:T(8,128)(2,1)}, bf16[512,128]{1,0:T(8,128)(2,1)S(1)}, u32[]{:S(2)}, u32[]{:S(2)}) collective-permute-start(bf16[512,128]{1,0:T(8,128)(2,1)} %bitcast.30), channel_id=1, source_target_pairs={{0,4},{4,0},{8,12},{12,8},{1,5},{5,1},{9,13},{13,9},{2,6},{6,2},{1... | collective-permute-start | bytes 393224 | tf_op jit(solution)/shard_map/ppermute | solution.py:410
  5.8 15.7 %collective-permute-start.2 = (bf16[512,128]{1,0:T(8,128)(2,1)}, bf16[512,128]{1,0:T(8,128)(2,1)S(1)}, u32[]{:S(2)}, u32[]{:S(2)}) collective-permute-start(bf16[512,128]{1,0:T(8,128)(2,1)} %bitcast.31), channel_id=1, source_target_pairs={{0,8},{4,12},{8,0},{12,4},{1,9},{5,13},{9,1},{13,5},{2,10},{6,14},... | collective-permute-start | bytes 393224 | tf_op jit(solution)/shard_map/ppermute | solution.py:410
  12.5 12.0 %collective-permute-start.1 = (bf16[432,128]{1,0:T(8,128)(2,1)S(1)}, bf16[432,128]{1,0:T(8,128)(2,1)S(1)}, u32[]{:S(2)}, u32[]{:S(2)}) collective-permute-start(bf16[432,128]{1,0:T(8,128)(2,1)S(1)} %get-tuple-element.28.refs_1_), channel_id=1, source_target_pairs={{0,12},{4,8},{8,4},{12,0},{1,13},{5,9},{9,5},{13,1},{2,14},{6,10},... | collective-permute-start | bytes 331784 | tf_op jit(solution)/shard_map/ppermute | solution.py:410
  23.8 6.6 %collective-permute-start.5 = (bf16[432,128]{1,0:T(8,128)(2,1)S(1)}, bf16[432,128]{1,0:T(8,128)(2,1)S(1)}, u32[]{:S(2)}, u32[]{:S(2)}) collective-permute-start(bf16[432,128]{1,0:T(8,128)(2,1)S(1)} %get-tuple-element.37), channel_id=1, source_target_pairs={{0,4},{4,0},{8,12},{12,8},{1,5},{5,1},{9,13},{13,9},{2,6},{6,2},{1... | collective-permute-start | bytes 331784 | tf_op jit(solution)/shard_map/ppermute | solution.py:410
  23.8 7.3 %collective-permute-start.4 = (bf16[432,128]{1,0:T(8,128)(2,1)S(1)}, bf16[432,128]{1,0:T(8,128)(2,1)S(1)}, u32[]{:S(2)}, u32[]{:S(2)}) collective-permute-start(bf16[432,128]{1,0:T(8,128)(2,1)S(1)} %get-tuple-element.37), channel_id=1, source_target_pairs={{0,8},{4,12},{8,0},{12,4},{1,9},{5,13},{9,1},{13,5},{2,10},{6,14},... | collective-permute-start | bytes 331784 | tf_op jit(solution)/shard_map/ppermute | solution.py:410

commit v3 on v2

--- a/solution.py
+++ b/solution.py
@@ -564,7 +564,7 @@
         _, sent, done = attend_pages(tuple(near), [arrived[x] for x in near], done)
         *state, done = join(own, [block_own, far], state, done, False)
         prefill_out, done = attend_source(EARLY, tiles, done, prefill_out)
-        dec_out = join(None, [swap(sent, x, instances) for x in near], state, done, True)
+        dec_out = join(None, [swap(sent, x, instances) for x in near[::-1]], state, done, True)
     else:
         queries = gather_all(queries)
         own, sent, done = attend_pages(None, [queries], state[0])

time: 33.1 us -> 32.2 us (0.973)
  Pallas kernels: 20.8 us -> 20.2 us
  waiting for transfers between devices: 0.72 us -> 0.31 us
    ppermute x6, waiting for transfers between devices: 0.72 us -> 0.31 us  [swap(): lax.ppermute(block, 'inst', [(i, i ^ offset) for i in range(instances)])]
  transfers between devices with their start and end apart: 6 -> 6, of which waited for: 1 -> 2; matrix products, arithmetic and copies ran while one was open for 0% -> 0% of each run, Pallas kernels for 57% -> 58%
where the time goes in v3:
time: 32.2 us; the launch traced here: 32.1 us
  Pallas kernels  20.2 us (63%)
  starting transfers between devices  10.3 us (32%)
  between operations  1.33 us (4%)
    ppermute x6, starting transfers between devices, swap(): lax.ppermute(block, 'inst', [(i, i ^ offset) for i in range(instances)])  10.3 us
    pallas_call x2, Pallas kernels, attend_source(): pl.pallas_call(functools.partial(prefill_kernel, (heads, page, pages, blo...  9.58 us
    pallas_call x2, Pallas kernels, attend_pages(): pl.pallas_call(functools.partial(pages_kernel, (heads, page, pages, rows,...  4.05 us
    pallas_call x1, Pallas kernels, shards(): pl.pallas_call(functools.partial(cache_kernel, sizes), out_shape=(shape((...  3.73 us
    pallas_call x2, Pallas kernels, join(): pl.pallas_call(functools.partial(join_kernel, (rows, requests, blocks_of)...  2.86 us
  transfers between devices with their start and end apart: 6, of which 2 were waited for; matrix products, arithmetic and copies ran while one was open for 0% of the time, Pallas kernels for 58%

profile of v3, /device:TPU:0, one launch (start us, length us, event | category | flops | bytes accessed | tf_op | source)
XLA Modules:
  0.0 32.1 jit_solution(4521548812085756092)
XLA Ops:
  0.6 0.0 copy-start
  0.6 5.1 %collective-permute-start = (bf16[512,128]{1,0:T(8,128)(2,1)}, bf16[512,128]{1,0:T(8,128)(2,1)S(1)}, u32[]{:S(2)}, u32[]{:S(2)}) collective-permute-start(bf16[512,128]{1,0:T(8,128)(2,1)} %bitcast.29), channel_id=1, source_target_pairs={{0,12},{4,8},{8,4},{12,0},{1,13},{5,9},{9,5},{13,1},{2,14},{6,10},... | collective-permute-start | bytes 393224 | tf_op jit(solution)/shard_map/ppermute | solution.py:410
  5.8 0.0 collective-permute-start.3
  5.8 0.6 %collective-permute-start.2 = (bf16[512,128]{1,0:T(8,128)(2,1)}, bf16[512,128]{1,0:T(8,128)(2,1)S(1)}, u32[]{:S(2)}, u32[]{:S(2)}) collective-permute-start(bf16[512,128]{1,0:T(8,128)(2,1)} %bitcast.31), channel_id=1, source_target_pairs={{0,8},{4,12},{8,0},{12,4},{1,9},{5,13},{9,1},{13,5},{2,10},{6,14},... | collective-permute-start | bytes 393224 | tf_op jit(solution)/shard_map/ppermute | solution.py:410
  7.1 3.7 %cache.1 = (s32[8,32]{1,0:T(8,128)S(1)}, f32[512,128]{1,0:T(8,128)S(1)}, f32[512,128]{1,0:T(8,128)S(1)}, f32[512,128]{1,0:T(8,128)S(1)}, bf16[768,256]{1,0:T(8,1...) custom-call(s32[1]{0:T(128)S(6)} %copy.19.len_ref, s32[1,24]{1,0:T(1,128)} %seg_hbm.1, ...), custom_call_target="tpu_custom_call" | custom-call | flops 1000 | bytes 1000 | tf_op jit(solution)/shard_map/cache/pallas_call | solution.py:465
  10.8 0.0 collective-permute-done.refs_1_
  10.8 1.7 %pages.2 = (f32[416,128]{1,0:T(8,128)S(1)}, bf16[432,128]{1,0:T(8,128)(2,1)S(1)}, f32[8,128]{1,0:T(8,128)S(1)}) custom-call(s32[8,32]{1,0:T(8,128)S(1)} %get-tuple-element.22.info_ref, bf16[512,128]{1,0:T(8,128)(2,1)S(1)} %get-tuple-element.25.refs_0_, bf16[512,128]{1,0:T(8,128)(2,1)S(1)} %collective-permute-done.refs_1_, ...), custom_call_target="tpu_custom_call" | custom-call | flops 1000 | bytes 1000 | tf_op jit(solution)/shard_map/pages/pallas_call | solution.py:493
  12.5 3.8 %collective-permute-start.1 = (bf16[432,128]{1,0:T(8,128)(2,1)S(1)}, bf16[432,128]{1,0:T(8,128)(2,1)S(1)}, u32[]{:S(2)}, u32[]{:S(2)}) collective-permute-start(bf16[432,128]{1,0:T(8,128)(2,1)S(1)} %get-tuple-element.28.refs_1_), channel_id=1, source_target_pairs={{0,12},{4,8},{8,4},{12,0},{1,13},{5,9},{9,5},{13,1},{2,14},{6,10},... | collective-permute-start | bytes 331784 | tf_op jit(solution)/shard_map/ppermute | solution.py:410
  16.3 0.0 copy-done
  16.3 5.1 %prefill.2 = (bf16[12288,128]{1,0:T(8,128)(2,1)}, f32[8,128]{1,0:T(8,128)S(1)}) custom-call(s32[8,32]{1,0:T(8,128)S(1)} %get-tuple-element.22.info_ref, bf16[12288,128]{1,0:T(8,128)(2,1)S(1)} %bitcast.24, bf16[768,256]{1,0:T(8,128)(2,1)S(1)} %get-tuple-element.23.refs_2_.keys_ref, bf16[768,256]{1,0:T(8,128)(2,1)S(1)} %get-tuple-element.24.refs_3_.vals_ref, ...), custom_call_target="tpu_custom_call" | custom-call | flops 1000 | bytes 1000 | tf_op jit(solution)/shard_map/prefill/pallas_call | solution.py:515
  21.4 0.0 collective-permute-done.3.refs_1_
  21.4 0.0 collective-permute-done.2.refs_0_
  21.4 2.4 %pages.3 = (f32[416,128]{1,0:T(8,128)}, bf16[432,128]{1,0:T(8,128)(2,1)S(1)}, f32[8,128]{1,0:T(8,128)S(1)}) custom-call(s32[8,32]{1,0:T(8,128)S(1)} %get-tuple-element.22.info_ref, bf16[512,128]{1,0:T(8,128)(2,1)S(1)} %collective-permute-done.2.refs_0_, bf16[512,128]{1,0:T(8,128)(2,1)S(1)} %collective-permute-done.3.refs_1_, ...), custom_call_target="tpu_custom_call" | custom-call | flops 1000 | bytes 1000 | tf_op jit(solution)/shard_map/pages/pallas_call | solution.py:493
  23.8 0.7 %collective-permute-start.5 = (bf16[432,128]{1,0:T(8,128)(2,1)S(1)}, bf16[432,128]{1,0:T(8,128)(2,1)S(1)}, u32[]{:S(2)}, u32[]{:S(2)}) collective-permute-start(bf16[432,128]{1,0:T(8,128)(2,1)S(1)} %get-tuple-element.37), channel_id=1, source_target_pairs={{0,8},{4,12},{8,0},{12,4},{1,9},{5,13},{9,1},{13,5},{2,10},{6,14},... | collective-permute-start | bytes 331784 | tf_op jit(solution)/shard_map/ppermute | solution.py:410
  24.5 0.0 collective-permute-start.4
  24.5 0.0 collective-permute-done.1.refs_2_
  24.5 1.2 %join.2 = (f32[512,128]{1,0:T(8,128)S(1)}, f32[512,128]{1,0:T(8,128)S(1)}, f32[512,128]{1,0:T(8,128)S(1)}, f32[8,128]{1,0:T(8,128)S(1)}) custom-call(f32[416,128]{1,0:T(8,128)S(1)} %get-tuple-element.27.refs_0_, bf16[432,128]{1,0:T(8,128)(2,1)S(1)} %get-tuple-element.28.refs_1_, bf16[432,128]{1,0:T(8,128)(2,1)S(1)} %collective-permute-done.1.refs_2_, ...), custom_call_target="tpu_custom_call" | custom-call | flops 1000 | bytes 1000 | tf_op jit(solution)/shard_map/join/pallas_call | solution.py:543
  25.7 4.5 %prefill.3 = (bf16[12288,128]{1,0:T(8,128)(2,1)}, f32[8,128]{1,0:T(8,128)S(1)}) custom-call(s32[8,32]{1,0:T(8,128)S(1)} %get-tuple-element.22.info_ref, bf16[12288,128]{1,0:T(8,128)(2,1)S(1)} %bitcast.25, bf16[768,256]{1,0:T(8,128)(2,1)S(1)} %get-tuple-element.23.refs_2_.keys_ref, ...), custom_call_target="tpu_custom_call", output_to_operand_aliasing={{0}: (5, {})} | custom-call | flops 1000 | bytes 1000 | tf_op jit(solution)/shard_map/prefill/pallas_call | solution.py:515
  30.1 0.2 collective-permute-done.5.refs_1_
  30.3 0.1 collective-permute-done.4.refs_0_
  30.4 1.7 %join.3 = bf16[512,128]{1,0:T(8,128)(2,1)} custom-call(bf16[432,128]{1,0:T(8,128)(2,1)S(1)} %collective-permute-done.4.refs_0_, bf16[432,128]{1,0:T(8,128)(2,1)S(1)} %collective-permute-done.5.refs_1_, f32[512,128]{1,0:T(8,128)S(1)} %get-tuple-element.38.refs_2_, f32[512,128]{1,0:T(8,128)S(1)} %get-tuple-element.39.refs_3_, ...), custom_call_target="tpu_custom_call" | custom-call | flops 1000 | bytes 1000 | tf_op jit(solution)/shard_map/join/pallas_call | solution.py:543
Async XLA Ops:
  0.6 15.7 %copy-start = (bf16[1,768,2,1024]{3,2,1,0:T(2,128)(2,1)S(1)}, bf16[1,768,2,1024]{3,2,1,0:T(2,128)(2,1)}, u32[]{:S(2)}) copy-start(bf16[1,768,2,1024]{3,2,1,0:T(2,128)(2,1)} %param.11) | copy-start | bytes 9437188
  0.6 10.1 %collective-permute-start = (bf16[512,128]{1,0:T(8,128)(2,1)}, bf16[512,128]{1,0:T(8,128)(2,1)S(1)}, u32[]{:S(2)}, u32[]{:S(2)}) collective-permute-start(bf16[512,128]{1,0:T(8,128)(2,1)} %bitcast.29), channel_id=1, source_target_pairs={{0,12},{4,8},{8,4},{12,0},{1,13},{5,9},{9,5},{13,1},{2,14},{6,10},... | collective-permute-start | bytes 393224 | tf_op jit(solution)/shard_map/ppermute | solution.py:410
  5.8 15.7 %collective-permute-start.3 = (bf16[512,128]{1,0:T(8,128)(2,1)}, bf16[512,128]{1,0:T(8,128)(2,1)S(1)}, u32[]{:S(2)}, u32[]{:S(2)}) collective-permute-start(bf16[512,128]{1,0:T(8,128)(2,1)} %bitcast.30), channel_id=1, source_target_pairs={{0,4},{4,0},{8,12},{12,8},{1,5},{5,1},{9,13},{13,9},{2,6},{6,2},{1... | collective-permute-start | bytes 393224 | tf_op jit(solution)/shard_map/ppermute | solution.py:410
  5.8 15.7 %collective-permute-start.2 = (bf16[512,128]{1,0:T(8,128)(2,1)}, bf16[512,128]{1,0:T(8,128)(2,1)S(1)}, u32[]{:S(2)}, u32[]{:S(2)}) collective-permute-start(bf16[512,128]{1,0:T(8,128)(2,1)} %bitcast.31), channel_id=1, source_target_pairs={{0,8},{4,12},{8,0},{12,4},{1,9},{5,13},{9,1},{13,5},{2,10},{6,14},... | collective-permute-start | bytes 393224 | tf_op jit(solution)/shard_map/ppermute | solution.py:410
  12.5 12.0 %collective-permute-start.1 = (bf16[432,128]{1,0:T(8,128)(2,1)S(1)}, bf16[432,128]{1,0:T(8,128)(2,1)S(1)}, u32[]{:S(2)}, u32[]{:S(2)}) collective-permute-start(bf16[432,128]{1,0:T(8,128)(2,1)S(1)} %get-tuple-element.28.refs_1_), channel_id=1, source_target_pairs={{0,12},{4,8},{8,4},{12,0},{1,13},{5,9},{9,5},{13,1},{2,14},{6,10},... | collective-permute-start | bytes 331784 | tf_op jit(solution)/shard_map/ppermute | solution.py:410
  23.8 6.5 %collective-permute-start.5 = (bf16[432,128]{1,0:T(8,128)(2,1)S(1)}, bf16[432,128]{1,0:T(8,128)(2,1)S(1)}, u32[]{:S(2)}, u32[]{:S(2)}) collective-permute-start(bf16[432,128]{1,0:T(8,128)(2,1)S(1)} %get-tuple-element.37), channel_id=1, source_target_pairs={{0,8},{4,12},{8,0},{12,4},{1,9},{5,13},{9,1},{13,5},{2,10},{6,14},... | collective-permute-start | bytes 331784 | tf_op jit(solution)/shard_map/ppermute | solution.py:410
  24.5 5.9 %collective-permute-start.4 = (bf16[432,128]{1,0:T(8,128)(2,1)S(1)}, bf16[432,128]{1,0:T(8,128)(2,1)S(1)}, u32[]{:S(2)}, u32[]{:S(2)}) collective-permute-start(bf16[432,128]{1,0:T(8,128)(2,1)S(1)} %get-tuple-element.37), channel_id=1, source_target_pairs={{0,4},{4,0},{8,12},{12,8},{1,5},{5,1},{9,13},{13,9},{2,6},{6,2},{1... | collective-permute-start | bytes 331784 | tf_op jit(solution)/shard_map/ppermute | solution.py:410
